TPU v7x, 256 devices: a whole 4x4x8 slice. The times are simulated.
256 devices in a mesh: dp: 4 (over z_lo, core), seq: 64 (over z_hi, x, y).
Axes of the slice: x: 4, y: 4, z: 8 (z_hi: 4, z_lo: 2; z = z_hi * 2 + z_lo), core: 2. Of those that a mesh axis runs over, the one named last changes fastest.
Arguments:
- tokens: bfloat16 [4, 65536, 768], P('dp', 'seq'), may hold values from -16 to 16
- first_factor: bfloat16 [256, 256, 256], P('seq'), may hold values from -0.375 to 0.375
- second_factor: bfloat16 [256, 256, 256], P('seq'), may hold values from -0.375 to 0.375
- value_weight: bfloat16 [768, 768], replicated, may hold values from -0.21875 to 0.21875
- gate_weight: bfloat16 [768, 768], replicated, may hold values from -0.21875 to 0.21875
- out_weight: bfloat16 [768, 768], replicated, may hold values from -0.21875 to 0.21875
- cotangent: bfloat16 [4, 65536, 768], P('dp', 'seq'), may hold values from -16 to 16
Outputs:
- result: bfloat16 [4, 65536, 768], P('dp', 'seq')
- grad_tokens: bfloat16 [4, 65536, 768], P('dp', 'seq')
- grad_first: float32 [256, 256, 256], P('seq')
- grad_second: float32 [256, 256, 256], P('seq')
- grad_value: float32 [768, 768], P('seq')
- grad_gate: float32 [768, 768], P('seq')
- grad_out: float32 [768, 768], P('seq')
All inputs are finite; a program needn't handle non-finite values.
Results may differ from a plain program's by a relative error of at most 0.014.
Values may be sent and summed in bfloat16 or wider, within the bound.
A program may use at most 128 MiB of HBM per device.

v0:
```python
import jax
import jax.numpy as jnp
from jax import lax
from jax.sharding import PartitionSpec as P


def contract_rows(left, right):
    return lax.dot_general(
        left, right, (((0,), (0,)), ((), ())), preferred_element_type=jnp.float32
    )


def contract_cols(left, right):
    return lax.dot_general(
        left, right, (((1,), (1,)), ((), ())), preferred_element_type=jnp.float32
    )


def shards(tokens, first_factor, second_factor, value_weight, gate_weight, out_weight, cotangent):
    a_local = first_factor.shape[0]
    width_b = first_factor.shape[1]
    b_local = second_factor.shape[0]
    width_a = second_factor.shape[1]
    width = tokens.shape[2]
    rows_in = tokens[0]
    value = jnp.dot(rows_in, value_weight, preferred_element_type=jnp.float32)
    gated = jnp.dot(rows_in, gate_weight, preferred_element_type=jnp.float32)
    sigma = jax.nn.sigmoid(gated)
    mixed_in = (value * sigma).astype(jnp.bfloat16)
    cube_in = mixed_in.reshape(a_local, width_b, width)
    first_pass = jnp.einsum(
        "apb,abd->apd", first_factor, cube_in, preferred_element_type=jnp.float32
    ).astype(jnp.bfloat16)
    piece = lax.all_to_all(first_pass, "seq", split_axis=1, concat_axis=0, tiled=True)
    mixed = jnp.einsum("pqa,apd->pqd", second_factor, piece, preferred_element_type=jnp.float32)
    received = piece
    second_pass = mixed.astype(jnp.bfloat16)
    flat_second = second_pass.reshape(b_local * width_a, width)
    result = jnp.dot(flat_second, out_weight, preferred_element_type=jnp.float32).astype(
        jnp.bfloat16
    )
    cot_rows = cotangent[0]
    back_second = (
        contract_cols(cot_rows, out_weight).astype(jnp.bfloat16).reshape(b_local, width_a, width)
    )
    out_term = contract_rows(flat_second, cot_rows)
    back_first = jnp.einsum(
        "pqa,pqd->apd", second_factor, back_second, preferred_element_type=jnp.float32
    ).astype(jnp.bfloat16)
    second_term = jnp.einsum(
        "pqd,apd->pqa", back_second, received, preferred_element_type=jnp.float32
    )
    piece = lax.all_to_all(back_first, "seq", split_axis=0, concat_axis=1, tiled=True)
    back_mixed = jnp.einsum("apb,apd->abd", first_factor, piece, preferred_element_type=jnp.float32)
    first_term = jnp.einsum("apd,abd->apb", piece, cube_in, preferred_element_type=jnp.float32)
    back_flat = back_mixed.reshape(a_local * width_b, width)
    dvalue = (back_flat * sigma).astype(jnp.bfloat16)
    dgate = (back_flat * value * sigma * (1.0 - sigma)).astype(jnp.bfloat16)
    grad_rows = (contract_cols(dvalue, value_weight) + contract_cols(dgate, gate_weight)).astype(
        jnp.bfloat16
    )
    value_term = contract_rows(rows_in, dvalue)
    gate_term = contract_rows(rows_in, dgate)
    stacked = jnp.stack([value_term, gate_term, out_term])
    shares = lax.psum_scatter(stacked, "seq", scatter_dimension=1, tiled=True)
    weights_sum, first_sum, second_sum = (
        lax.psum(shares.astype(jnp.bfloat16), "dp").astype(jnp.float32),
        lax.psum(first_term.astype(jnp.bfloat16), "dp").astype(jnp.float32),
        lax.psum(second_term.astype(jnp.bfloat16), "dp").astype(jnp.float32),
    )
    return (
        result[None],
        grad_rows[None],
        first_sum,
        second_sum,
        weights_sum[0],
        weights_sum[1],
        weights_sum[2],
    )


def solution(mesh):
    return jax.shard_map(
        shards,
        mesh=mesh,
        in_specs=(
            P("dp", "seq", None),
            P("seq", None, None),
            P("seq", None, None),
            P(),
            P(),
            P(),
            P("dp", "seq", None),
        ),
        out_specs=(
            P("dp", "seq", None),
            P("dp", "seq", None),
            P("seq", None, None),
            P("seq", None, None),
            P("seq", None),
            P("seq", None),
            P("seq", None),
        ),
        check_vma=False,
    )
```

profile of v0, /device:TPU:1, one launch (start us, length us, event | category | flops | bytes accessed | tf_op | source)
XLA Modules:
  0.0 666.1 jit_solution(16359445861283507708)
XLA Ops:
  7.2 0.0 copy-start
  7.2 0.0 copy-start.6
  7.2 3.3 convolution_convert_fusion.3
  10.5 0.0 copy-start.8
  10.5 1.2 copy-done.8
  11.7 0.0 copy-done.6
  11.7 0.7 fusion.14
  12.4 2.2 copy.38
  14.6 15.1 %all-to-all-start.1 = ((bf16[256,4,768]{2,1,0:T(4,128)(2,1)}), bf16[256,4,768]{2,1,0:T(4,128)(2,1)S(1)}, u32[]{:S(2)}, u32[]{:S(2)}) async-start(bf16[256,4,768]{2,1,0:T(4,128)(2,1)} %copy.38), calls=%async_computation.1 | async-start | bytes 3145728 | tf_op jit(solution)/shard_map/all_to_all | solution.py:53
  29.8 0.0 copy-done
  29.8 4.3 fusion.9
  34.1 31.9 %all-to-all-done.1 = bf16[256,4,768]{2,1,0:T(4,128)(2,1)S(1)} async-done(((bf16[256,4,768]{2,1,0:T(4,128)(2,1)}), bf16[256,4,768]{2,1,0:T(4,128)(2,1)S(1)}, u32[]{:S(2)}, u32[]{:S(2)}) %all-to-all-start.1) | async-done | bytes 1572896 | tf_op jit(solution)/shard_map/all_to_all | solution.py:53
  66.0 1.7 copy.39
  67.7 2.7 all_to_all.33
  70.4 0.0 copy-start.2
  70.4 0.0 copy-start.14
  70.5 0.0 copy-start.19
  70.5 2.2 fusion.16
  72.7 0.0 copy-done.2
  72.7 0.0 copy-done.14
  72.7 0.7 copy-done.19
  73.4 3.7 fusion.3
  77.2 1.2 copy-done.11
  78.3 0.0 copy-done.5
  78.3 0.7 fusion.13
  79.1 2.3 copy.35
  81.4 11.0 %all-to-all-start = ((bf16[4,256,768]{2,0,1:T(4,128)(2,1)}), bf16[4,256,768]{2,0,1:T(4,128)(2,1)S(1)}, u32[]{:S(2)}, u32[]{:S(2)}) async-start(bf16[4,256,768]{2,0,1:T(4,128)(2,1)} %copy.35), calls=%async_computation | async-start | bytes 3145728 | tf_op jit(solution)/shard_map/all_to_all | solution.py:34
  92.4 0.2 all-reduce.5.cloned.1.call-start
  92.6 0.0 copy-done.17
  92.6 0.6 dynamic-slice
  93.9 0.0 copy-start.13
  93.9 0.0 copy-start.20
  93.9 3.4 convolution_convert_fusion.6
  97.3 0.0 copy-done.13
  97.3 0.0 copy-done.20
  97.3 1.4 fusion.17
  98.8 0.0 copy-start.18
  98.8 2.9 convolution_bitcast_fusion.2
  101.7 0.0 copy-done.18
  101.7 2.9 convolution_bitcast_fusion.1
  104.6 0.0 copy-done.15
  104.6 2.6 fusion.12
  107.1 25.0 %all-to-all-done = bf16[4,256,768]{2,0,1:T(4,128)(2,1)S(1)} async-done(((bf16[4,256,768]{2,0,1:T(4,128)(2,1)}), bf16[4,256,768]{2,0,1:T(4,128)(2,1)S(1)}, u32[]{:S(2)}, u32[]{:S(2)}) %all-to-all-start) | async-done | bytes 1572896 | tf_op jit(solution)/shard_map/all_to_all | solution.py:34
  132.1 1.7 copy.36
  133.8 2.8 all_to_all.29
  136.6 0.0 copy-done.7
  136.6 0.0 copy-start.9
  136.6 1.7 convolution_convert_fusion
  138.3 1.4 convolution_convert_fusion.5
  139.7 0.0 copy-done.10
  139.8 3.0 convolution_bitcast_fusion
  142.8 3.3 pad_maximum_fusion
  146.1 11.0 %copy.42 = f32[3,768,768]{2,0,1:T(4,128)} copy(f32[3,768,768]{1,2,0:T(8,128)} %pad_maximum_fusion) | data formatting | bytes 14155776 | tf_op jit(solution)/shard_map/stack | solution.py:64
  157.1 0.0 all-reduce.5.cloned.1.call-update
  157.1 0.0 copy-start.16
  157.2 464.4 %all-reduce.6 = bf16[3,768,768]{2,0,1:T(4,128)(2,1)} all-reduce(f32[3,768,768]{2,0,1:T(4,128)} %copy.42), channel_id=2, replica_groups=mesh['dp'=4,'seq'=64] {'seq'}, use_global_device_ids=true, to_apply=%region_2.0.clone | all-reduce | flops 1769472 | bytes 10616832
  621.5 0.9 dynamic-slice_convert_fusion
  622.5 29.6 %psum.23 = bf16[3,12,768]{2,0,1:T(4,128)(2,1)S(1)} all-reduce(bf16[3,12,768]{2,0,1:T(4,128)(2,1)S(1)} %dynamic-slice_convert_fusion), channel_id=1, replica_groups=mesh['dp'=4,'seq'=64] {'dp'}, use_global_device_ids=true, to_apply=%region_3.0 | all-reduce | flops 27648 | bytes 110592 | tf_op jit(solution)/shard_map/psum | solution.py:67
  652.0 0.1 fusion.15
  652.1 0.6 copy.53
  652.8 0.6 copy_bitcast_fusion
  653.4 2.5 fusion.11
  655.9 2.2 convert_element_type.67
  658.2 1.1 convert_element_type.69
  (17 shorter events, 0.0 us)
Async XLA Ops:
  7.2 22.6 %copy-start = (bf16[1,1024,768]{2,1,0:T(8,128)(2,1)S(1)}, bf16[1,1024,768]{2,1,0:T(8,128)(2,1)}, u32[]{:S(2)}) copy-start(bf16[1,1024,768]{2,1,0:T(8,128)(2,1)} %param.7) | copy-start | bytes 4718596
  7.2 4.5 copy-start.6
  10.5 1.2 copy-start.8
  14.6 51.4 %all-to-all-start.1 = ((bf16[256,4,768]{2,1,0:T(4,128)(2,1)}), bf16[256,4,768]{2,1,0:T(4,128)(2,1)S(1)}, u32[]{:S(2)}, u32[]{:S(2)}) async-start(bf16[256,4,768]{2,1,0:T(4,128)(2,1)} %copy.38), calls=%async_computation.1 | async-start | bytes 3145728 | tf_op jit(solution)/shard_map/all_to_all | solution.py:53
  70.4 2.3 copy-start.2
  70.4 2.3 copy-start.14
  70.5 3.0 copy-start.19
  73.4 4.9 copy-start.5
  77.2 1.2 copy-start.11
  81.4 11.2 %copy-start.17 = (u32[256]{0:T(256)S(1)}, u32[256]{0:T(256)}, u32[]{:S(2)}) copy-start(u32[256]{0:T(256)} %constant.8) | copy-start | bytes 3076
  81.4 50.7 %all-to-all-start = ((bf16[4,256,768]{2,0,1:T(4,128)(2,1)}), bf16[4,256,768]{2,0,1:T(4,128)(2,1)S(1)}, u32[]{:S(2)}, u32[]{:S(2)}) async-start(bf16[4,256,768]{2,0,1:T(4,128)(2,1)} %copy.35), calls=%async_computation | async-start | bytes 3145728 | tf_op jit(solution)/shard_map/all_to_all | solution.py:34
  92.4 563.6 %all-reduce.5.cloned.1.call-start = ((), (), s32[]{:S(2)}) async-start(), calls=%async_computation.2 | async-start | bytes 2097152 | tf_op jit(solution)/shard_map/psum | solution.py:68
  93.9 3.5 copy-start.13
  93.9 3.5 copy-start.20
  98.8 2.9 copy-start.18
  101.7 2.9 copy-start.15
  133.8 2.8 copy-start.7
  136.6 1.7 copy-start.9
  138.3 1.4 copy-start.10
  139.7 3.1 copy-start.3
  139.7 3.1 copy-start.4
  157.1 496.2 %copy-start.16 = (bf16[768,768]{1,0:T(8,128)(2,1)S(1)}, bf16[768,768]{1,0:T(8,128)(2,1)}, u32[]{:S(2)}) copy-start(bf16[768,768]{1,0:T(8,128)(2,1)} %param.12) | copy-start | bytes 3538948
  655.9 2.3 copy-start.12
  655.9 3.3 copy-start.1
Sparse Core Ops, SparseCore 0:
  157.3 73.9 all-reduce.4
where the time goes:
time: 667 us; the launch traced here: 666 us
  blocking collectives  494 us (74%)
  waiting for transfers between devices  56.9 us (9%)
  matrix products  36.9 us (6%)
  local copies, waits for them, and re-layouts  30.4 us (5%)
  starting transfers between devices  26.3 us (4%)
  between operations  14.9 us (2%)
    unnamed x1, blocking collectives  464 us
    all_to_all x1, waiting for transfers between devices, shards(): lax.all_to_all(back_first, 'seq', split_axis=0, concat_axis=1, tiled=True)  31.9 us
    psum x1, blocking collectives, shards(): lax.psum(shares.astype(jnp.bfloat16), 'dp').astype(jnp.float32)  29.6 us
    all_to_all x1, waiting for transfers between devices, shards(): lax.all_to_all(first_pass, 'seq', split_axis=1, concat_axis=0, tiled=True)  25 us
    all_to_all x1, starting transfers between devices, shards(): lax.all_to_all(back_first, 'seq', split_axis=0, concat_axis=1, tiled=True)  15.1 us
  transfers between devices with their start and end apart: 3, of which 2 were waited for; matrix products, arithmetic and copies ran while one was open for 3% of the time, Pallas kernels for 0%

commit v1 on v0

v1 whole, which is shorter than its diff:
```python
import jax
import jax.numpy as jnp
from jax import lax
from jax.experimental import pallas as pl
from jax.experimental.pallas import tpu as pltpu
from jax.sharding import PartitionSpec as P

MESH = pl.DeviceIdType.MESH
BF16 = jnp.bfloat16
F32 = jnp.float32


def contract_rows(left, right):
    return lax.dot_general(left, right, (((0,), (0,)), ((), ())), preferred_element_type=F32)


def contract_cols(left, right):
    return lax.dot_general(left, right, (((1,), (1,)), ((), ())), preferred_element_type=F32)


def exchange_kernel(a_ref, b_ref, a_out, b_out, send_sem, recv_sem):
    dp, seq = lax.axis_index("dp"), lax.axis_index("seq")
    barrier = pltpu.get_barrier_semaphore()

    def peer(step):
        return lax.rem(seq + step, 64)

    def greet(step, carry):
        pl.semaphore_signal(barrier, inc=1, device_id=(dp, peer(step)), device_id_type=MESH)
        return carry

    lax.fori_loop(1, 64, greet, 0)
    pl.semaphore_wait(barrier, 63)
    for k, (src, dst) in enumerate(((a_ref, a_out), (b_ref, b_out))):

        def send(step, carry, src=src, dst=dst, k=k):
            pltpu.make_async_remote_copy(
                src_ref=src.at[peer(step)],
                dst_ref=dst.at[seq],
                send_sem=send_sem.at[k],
                recv_sem=recv_sem.at[k],
                device_id=(dp, peer(step)),
                device_id_type=MESH,
            ).start()
            return carry

        lax.fori_loop(1, 64, send, 0)
        dst[seq] = src[seq]
    for k, (src, dst) in enumerate(((a_ref, a_out), (b_ref, b_out))):
        whole = pltpu.make_async_remote_copy(
            src_ref=src.at[pl.ds(0, 63)],
            dst_ref=dst.at[pl.ds(0, 63)],
            send_sem=send_sem.at[k],
            recv_sem=recv_sem.at[k],
            device_id=(dp, peer(1)),
            device_id_type=MESH,
        )
        whole.wait_send()
        whole.wait_recv()


def exchange(a, b):
    shape = jax.ShapeDtypeStruct((64, 16, 768), BF16)
    vmem = pl.BlockSpec(memory_space=pltpu.VMEM)
    return pl.pallas_call(
        exchange_kernel,
        out_shape=(shape, shape),
        in_specs=[vmem] * 2,
        out_specs=(vmem, vmem),
        scratch_shapes=[pltpu.SemaphoreType.DMA((2,)), pltpu.SemaphoreType.DMA((2,))],
        compiler_params=pltpu.CompilerParams(
            collective_id=0, has_side_effects=True, vmem_limit_bytes=32 * 2**20
        ),
        name="exchange",
    )(a, b)


def reduce_kernel(
    w_ref, f_ref, w_out, f_out, w_r0, u, r1, wsum, r2, f_r0, f_s, f_r1, f_t, send_sem, recv_sem
):
    dp, seq = lax.axis_index("dp"), lax.axis_index("seq")
    zl, core = dp // 2, lax.rem(dp, 2)
    zh, xy = seq // 16, lax.rem(seq, 16)
    z = zh * 2 + zl
    other = 1 - core
    barrier = pltpu.get_barrier_semaphore()

    def copy(src, dst, k, device):
        return pltpu.make_async_remote_copy(
            src_ref=src,
            dst_ref=dst,
            send_sem=send_sem.at[k],
            recv_sem=recv_sem.at[k],
            device_id=device,
            device_id_type=MESH,
        )

    def plane(step):
        to = lax.rem(xy + step, 16)
        return to, (dp, zh * 16 + to)

    def column(step):
        to = lax.rem(z * 2 + core + step, 16)
        to_z, to_core = to // 2, lax.rem(to, 2)
        return to_z // 2, (lax.rem(to_z, 2) * 2 + to_core, (to_z // 2) * 16 + xy)

    def greet(step, carry):
        pl.semaphore_signal(barrier, inc=1, device_id=plane(step)[1], device_id_type=MESH)
        pl.semaphore_signal(barrier, inc=1, device_id=column(step)[1], device_id_type=MESH)
        return carry

    lax.fori_loop(1, 16, greet, 0)
    pl.semaphore_wait(barrier, 30)
    partner = (zl * 2 + other, seq)
    neighbour = ((1 - zl) * 2 + core, seq)

    s0 = copy(w_ref.at[other], w_r0, 0, partner)
    s0.start()
    g0 = copy(f_ref.at[other], f_r0, 1, partner)
    g0.start()
    s0.wait()

    def add_pair(i, carry):
        u[i] = (w_ref[core, i].astype(F32) + w_r0[i].astype(F32)).astype(BF16)
        return carry

    lax.fori_loop(0, 16, add_pair, 0)

    def send_plane(step, carry):
        to, device = plane(step)
        copy(u.at[to], r1.at[xy], 2, device).start()
        return carry

    lax.fori_loop(1, 16, send_plane, 0)
    r1[xy] = u[xy]
    g0.wait()

    def add_factor(i, carry):
        rows = pl.ds(pl.multiple_of(i * 128, 128), 128)
        f_s[rows, :] = (f_ref[core, rows, :].astype(F32) + f_r0[rows, :].astype(F32)).astype(BF16)
        return carry

    lax.fori_loop(0, 8, add_factor, 0)
    g1 = copy(f_s, f_r1, 3, neighbour)
    g1.start()
    copy(u.at[pl.ds(0, 15)], r1.at[pl.ds(0, 15)], 2, plane(1)[1]).wait()

    def add_plane(q, carry):
        total = r1[0, q].astype(F32)
        for i in range(1, 16):
            total = total + r1[i, q].astype(F32)
        wsum[q] = total.astype(BF16)
        return carry

    lax.fori_loop(0, 4, add_plane, 0)

    def send_column(step, carry):
        to, device = column(step)
        copy(wsum.at[to], r2.at[core * 8 + z], 4, device).start()
        return carry

    lax.fori_loop(1, 16, send_column, 0)
    r2[core * 8 + z] = wsum[zh]
    g1.wait()

    def add_neighbour(i, carry):
        rows = pl.ds(pl.multiple_of(i * 128, 128), 128)
        f_t[core, rows, :] = (f_s[rows, :].astype(F32) + f_r1[rows, :].astype(F32)).astype(BF16)
        return carry

    lax.fori_loop(0, 8, add_neighbour, 0)
    g2 = copy(f_t.at[core], f_t.at[core], 5, partner)
    g2.start()
    copy(r2.at[pl.ds(0, 15)], r2.at[pl.ds(0, 15)], 4, partner).wait()
    for half in range(2):
        total = r2[half * 8].astype(F32)
        for i in range(1, 8):
            total = total + r2[half * 8 + i].astype(F32)
        w_out[:, half * 384 : (half + 1) * 384] = total
    g2.wait()
    f_out[...] = f_t[...].astype(F32)


def reduce_all(w, f):
    vmem = pl.BlockSpec(memory_space=pltpu.VMEM)
    return pl.pallas_call(
        reduce_kernel,
        out_shape=(
            jax.ShapeDtypeStruct((48, 768), F32),
            jax.ShapeDtypeStruct((2, 1024, 256), F32),
        ),
        in_specs=[vmem] * 2,
        out_specs=(vmem, vmem),
        scratch_shapes=[
            pltpu.VMEM((16, 4, 48, 384), BF16),
            pltpu.VMEM((16, 4, 48, 384), BF16),
            pltpu.VMEM((16, 4, 48, 384), BF16),
            pltpu.VMEM((4, 48, 384), BF16),
            pltpu.VMEM((16, 48, 384), BF16),
            pltpu.VMEM((1024, 256), BF16),
            pltpu.VMEM((1024, 256), BF16),
            pltpu.VMEM((1024, 256), BF16),
            pltpu.VMEM((2, 1024, 256), BF16),
            pltpu.SemaphoreType.DMA((6,)),
            pltpu.SemaphoreType.DMA((6,)),
        ],
        compiler_params=pltpu.CompilerParams(
            collective_id=1, has_side_effects=True, vmem_limit_bytes=40 * 2**20
        ),
        name="reduce",
    )(w, f)


def shards(tokens, first_factor, second_factor, value_weight, gate_weight, out_weight, cotangent):
    rows_in = tokens[0]
    cot_rows = cotangent[0]
    back_second = contract_cols(cot_rows, out_weight).astype(BF16).reshape(4, 256, 768)
    back_first = jnp.einsum(
        "pqa,pqd->apd", second_factor, back_second, preferred_element_type=F32
    ).astype(BF16)
    value = jnp.dot(rows_in, value_weight, preferred_element_type=F32)
    gated = jnp.dot(rows_in, gate_weight, preferred_element_type=F32)
    sigma = jax.nn.sigmoid(gated)
    cube_in = (value * sigma).astype(BF16).reshape(4, 256, 768)
    first_pass = jnp.einsum(
        "apb,abd->pad", first_factor, cube_in, preferred_element_type=F32
    ).astype(BF16)
    back_got, first_got = exchange(
        back_first.reshape(64, 16, 768), first_pass.reshape(64, 16, 768)
    )
    back_cube = back_got.reshape(64, 4, 4, 768)
    first_cube = first_got.reshape(64, 4, 4, 768)
    piece = back_cube.transpose(1, 0, 2, 3).reshape(4, 256, 768)
    back_mixed = jnp.einsum("apb,apd->abd", first_factor, piece, preferred_element_type=F32)
    first_term = jnp.einsum("apd,abd->apb", piece, cube_in, preferred_element_type=F32)
    back_flat = back_mixed.reshape(1024, 768)
    dvalue = (back_flat * sigma).astype(BF16)
    dgate = (back_flat * value * sigma * (1.0 - sigma)).astype(BF16)
    grad_rows = (contract_cols(dvalue, value_weight) + contract_cols(dgate, gate_weight)).astype(
        BF16
    )
    value_term = contract_rows(rows_in, dvalue)
    gate_term = contract_rows(rows_in, dgate)
    received = first_cube.transpose(1, 0, 2, 3).reshape(4, 256, 768)
    second_pass = jnp.einsum(
        "pqa,pad->pqd", second_factor, received, preferred_element_type=F32
    ).astype(BF16)
    flat_second = second_pass.reshape(1024, 768)
    result = jnp.dot(flat_second, out_weight, preferred_element_type=F32).astype(BF16)
    out_term = contract_rows(flat_second, cot_rows)
    second_term = jnp.einsum("pqd,pad->pqa", back_second, received, preferred_element_type=F32)
    w = jnp.stack([value_term, gate_term, out_term]).astype(BF16)
    w = jnp.pad(w.reshape(3, 4, 16, 12, 2, 384), ((0, 0), (0, 0), (0, 0), (0, 4), (0, 0), (0, 0)))
    w = w.transpose(4, 2, 1, 0, 3, 5).reshape(2, 16, 4, 48, 384)
    f = jnp.stack([first_term, second_term]).astype(BF16).reshape(2, 2, 512, 256)
    f = f.transpose(1, 0, 2, 3).reshape(2, 1024, 256)
    w_sum, f_sum = reduce_all(w, f)
    w_sum = w_sum.reshape(3, 16, 768)[:, :12]
    f_sum = f_sum.reshape(2, 2, 512, 256).transpose(1, 0, 2, 3).reshape(2, 4, 256, 256)
    return (
        result[None],
        grad_rows[None],
        f_sum[0],
        f_sum[1],
        w_sum[0],
        w_sum[1],
        w_sum[2],
    )


def solution(mesh):
    return jax.shard_map(
        shards,
        mesh=mesh,
        in_specs=(
            P("dp", "seq", None),
            P("seq", None, None),
            P("seq", None, None),
            P(),
            P(),
            P(),
            P("dp", "seq", None),
        ),
        out_specs=(
            P("dp", "seq", None),
            P("dp", "seq", None),
            P("seq", None, None),
            P("seq", None, None),
            P("seq", None),
            P("seq", None),
            P("seq", None),
        ),
        check_vma=False,
    )
```

time: 667 us -> 261 us (0.39)
  the two profiles are of different devices: /device:TPU:1 before, /device:TPU:93 now
where the time goes in v1:
time: 261 us; the launch traced here: 260 us
  Pallas kernels  158 us (61%)
  local copies, waits for them, and re-layouts  62.6 us (24%)
  matrix products  35.9 us (14%)
  other arithmetic  2.61 us (1%)
    pallas_call x1, Pallas kernels, reduce_all(): pl.pallas_call(reduce_kernel, out_shape=(jax.ShapeDtypeStruct((48, 768),...  80.7 us
    pallas_call x1, Pallas kernels, exchange(): pl.pallas_call(exchange_kernel, out_shape=(shape, shape), in_specs=[vmem]...  77 us
    another operation x4, local copies, waits for them, and re-layouts, shards(): w = jnp.stack([value_term, gate_term, out_term]).astype(BF16)  11.4 us
    unnamed x54, local copies, waits for them, and re-layouts  10.2 us
    dot_general x3, matrix products, contract_rows(): lax.dot_general(left, right, (((0,), (0,)), ((), ())), preferred_element_...  10.1 us
    dot_general x3, local copies, waits for them, and re-layouts, contract_rows(): lax.dot_general(left, right, (((0,), (0,)), ((), ())), preferred_element_...  7.51 us
    dot_general x3, matrix products, contract_cols(): lax.dot_general(left, right, (((1,), (1,)), ((), ())), preferred_element_...  6.75 us

profile of v1, /device:TPU:93, one launch (start us, length us, event | category | flops | bytes accessed | tf_op | source)
XLA Modules:
  0.0 259.8 jit_solution(17874228742995906511)
XLA Ops:
  0.6 0.0 copy-start
  0.7 2.8 %copy.48 = bf16[768,1024]{1,0:T(8,128)(2,1)} copy(bf16[768,1024]{0,1:T(8,128)(2,1)} %bitcast.127) | data formatting | bytes 3145728 | tf_op jit(solution)/shard_map/dot_general | solution.py:14
  3.4 2.7 %convolution_convert_fusion.4 = bf16[1024,768]{1,0:T(8,128)(2,1)S(1)} fusion(bf16[768,768]{1,0:T(8,128)(2,1)} %param.12, bf16[1,1024,768]{2,1,0:T(8,128)(2,1)S(1)} %copy-done.21), kind=kOutput, calls=%fused_computation.20 | convolution fusion | flops 1208745984 | bytes 4325376 | tf_op jit(solution)/shard_map/dot_general | solution.py:18
  6.2 0.6 fusion.31
  6.8 0.5 copy-done.20
  7.3 2.4 copy.27
  9.7 2.7 %reshape.86.a_ref = bf16[64,16,768]{2,1,0:T(8,128)(2,1)S(1)} reshape(bf16[256,4,768]{2,1,0:T(4,128)(2,1)} %copy.27) | data formatting | bytes 3145728 | tf_op jit(solution)/shard_map/reshape | solution.py:229
  12.4 0.0 copy-start.22
  12.4 3.0 %add_divide_fusion = f32[1024,768]{1,0:T(8,128)S(1)} fusion(bf16[768,768]{1,0:T(8,128)(2,1)} %param.11, bf16[1,1024,768]{2,1,0:T(8,128)(2,1)S(1)} %copy-done), kind=kOutput, calls=%fused_computation.15 | convolution fusion | flops 1210318848 | bytes 5898240 | tf_op jit(solution)/shard_map/dot_general | solution.py:222
  15.5 0.0 copy-start.14
  15.5 3.1 %multiply_convert_fusion = (bf16[1024,768]{1,0:T(8,128)(2,1)S(1)}, f32[1024,768]{1,0:T(8,128)}) fusion(f32[1024,768]{1,0:T(8,128)S(1)} %add_divide_fusion, bf16[768,768]{1,0:T(8,128)(2,1)S(1)} %copy-done.22, bf16[1,1024,768]{2,1,0:T(8,128)(2,1)S(1)} %copy-done), kind=kOutput, calls=%fused_computation.14 | convolution fusion | flops 1209532416 | bytes 10616832 | tf_op jit(solution)/shard_map/dot_general | solution.py:221
  18.7 0.0 copy-done.14
  18.7 0.6 fusion.32
  19.2 0.6 copy-done.10
  19.8 2.4 copy.28
  22.2 3.7 %reshape.88.b_ref = bf16[64,16,768]{2,1,0:T(8,128)(2,1)} reshape(bf16[256,4,768]{2,1,0:T(4,128)(2,1)} %copy.28) | data formatting | bytes 3145728 | tf_op jit(solution)/shard_map/reshape | solution.py:229
  25.9 1.4 copy-done.1
  27.3 77.0 %exchange.1 = (bf16[64,16,768]{2,1,0:T(8,128)(2,1)S(1)}, bf16[64,16,768]{2,1,0:T(8,128)(2,1)S(1)}) custom-call(bf16[64,16,768]{2,1,0:T(8,128)(2,1)S(1)} %reshape.86.a_ref, bf16[64,16,768]{2,1,0:T(8,128)(2,1)S(1)} %copy-done.1), custom_call_target="tpu_custom_call" | custom-call | tf_op jit(solution)/shard_map/exchange/pallas_call | solution.py:65
  104.3 1.2 copy-done.2
  105.5 1.1 copy-done.4
  106.6 2.9 %reshape.89 = bf16[64,4,4,768]{3,2,1,0:T(4,128)(2,1)S(1)} reshape(bf16[64,16,768]{2,1,0:T(8,128)(2,1)} %copy-done.4) | data formatting | bytes 3145728 | tf_op jit(solution)/shard_map/reshape | solution.py:232
  109.5 1.7 copy.29
  111.2 2.9 %reshape.90 = bf16[4,256,768]{2,1,0:T(8,128)(2,1)S(1)} reshape(bf16[4,64,4,768]{3,2,1,0:T(4,128)(2,1)} %copy.29) | data formatting | bytes 3145728 | tf_op jit(solution)/shard_map/reshape | solution.py:244
  114.2 0.0 copy-start.13
  114.2 2.9 %convolution_convert_fusion.5 = bf16[4,256,256]{2,1,0:T(8,128)(2,1)} fusion(bf16[4,256,768]{2,1,0:T(8,128)(2,1)} %bitcast.126, bf16[4,256,768]{2,1,0:T(8,128)(2,1)S(1)} %reshape.90), kind=kOutput, calls=%fused_computation.41 | convolution fusion | flops 402915328 | bytes 3670016 | tf_op jit(solution)/shard_map/pqd,pad->pqa/dot_general | solution.py:251
  117.0 1.7 convolution_convert_fusion
  118.8 2.7 %copy.34 = bf16[1024,768]{0,1:T(8,128)(2,1)} copy(bf16[1024,768]{1,0:T(8,128)(2,1)} %bitcast.117) | data formatting | bytes 3145728 | tf_op jit(solution)/shard_map/reshape | solution.py:248
  121.5 3.8 %fusion.29 = bf16[1,1024,768]{2,1,0:T(8,128)(2,1)} fusion(bf16[1024,768]{1,0:T(8,128)(2,1)S(1)} %bitcast.118, bf16[768,768]{1,0:T(8,128)(2,1)} %param.12), kind=kOutput, calls=%fused_computation.34 | convolution fusion | flops 1208745984 | bytes 4325376 | tf_op jit(solution)/shard_map/dot_general | solution.py:249
  125.3 3.6 %reshape.95 = bf16[4,16,12,1024]{3,2,1,0:T(8,128)(2,1)} reshape(bf16[768,1024]{1,0:T(8,128)(2,1)} %bitcast.119) | data formatting | bytes 3145728 | tf_op jit(solution)/shard_map/reshape.16
  128.9 5.1 %fusion.33 = bf16[1,4,16,12,2,384]{5,2,4,3,1,0:T(8,128)(2,1)} fusion(bf16[2,384,1024,1,1]{2,1,0,4,3:T(8,128)(2,1)} %bitcast.128, bf16[4,16,12,1024,1]{3,2,1,0,4:T(8,128)(2,1)} %bitcast.124), kind=kOutput, calls=%fused_computation.38 | convolution fusion | flops 1208549376 | bytes 4325376 | tf_op jit(solution)/shard_map/dot_general | solution.py:14
  134.0 1.3 reshape.92
  135.4 1.9 copy.30
  137.3 1.3 reshape.93
  138.7 2.6 %convolution_convert_fusion.6 = bf16[4,256,256]{2,1,0:T(8,128)(2,1)S(1)} fusion(bf16[4,256,768]{2,1,0:T(8,128)(2,1)} %reshape.93, bf16[4,256,768]{2,1,0:T(8,128)(2,1)} %bitcast.123), kind=kOutput, calls=%fused_computation.42 | convolution fusion | flops 402915328 | bytes 3670016 | tf_op jit(solution)/shard_map/apd,abd->apb/dot_general | solution.py:235
  141.3 0.0 copy-start.15
  141.3 0.1 pad_maximum_fusion
  141.4 0.0 copy-done.9
  141.4 0.9 copy-done.15
  142.3 0.6 fusion.43
  143.0 0.4 copy-done.7
  143.4 1.2 copy-done.6
  144.5 2.0 fusion.9
  146.5 1.2 copy-done.16
  147.7 2.5 fusion.36
  150.2 2.4 copy.33
  152.5 3.6 %stack.20 = bf16[1,4,16,12,2,384]{5,4,3,2,1,0:T(2,128)(2,1)} reshape(bf16[768,768]{1,0:T(8,128)(2,1)} %copy.33) | data formatting | bytes 2359296 | tf_op jit(solution)/shard_map/stack | solution.py:252
  156.1 2.6 %copy.38 = bf16[1,4,16,12,2,384]{5,2,4,3,1,0:T(8,128)(2,1)} copy(bf16[1,4,16,12,2,384]{5,4,3,2,1,0:T(2,128)(2,1)} %stack.20) | data formatting | bytes 2359296 | tf_op jit(solution)/shard_map/stack | solution.py:252
  158.7 0.0 copy-done.18
  158.7 2.5 fusion.39
  161.2 2.4 copy.32
  163.6 3.6 %stack.19 = bf16[1,4,16,12,2,384]{5,4,3,2,1,0:T(2,128)(2,1)} reshape(bf16[768,768]{1,0:T(8,128)(2,1)} %copy.32) | data formatting | bytes 2359296 | tf_op jit(solution)/shard_map/stack | solution.py:252
  167.2 1.6 copy.37
  168.8 0.0 copy-done.11
  168.8 0.4 copy-done.24
  169.2 0.6 fusion.5
  169.8 1.8 copy.39
  171.6 80.7 %reduce.1 = (f32[48,768]{1,0:T(8,128)S(1)}, f32[2,1024,256]{2,1,0:T(8,128)S(1)}) custom-call(bf16[2,16,4,48,384]{4,3,2,1,0:T(8,128)(2,1)S(1)} %bitcast.113, bf16[2,1024,256]{2,1,0:T(8,128)(2,1)S(1)} %bitcast.114), custom_call_target="tpu_custom_call" | custom-call | tf_op jit(solution)/shard_map/reduce/pallas_call | solution.py:186
  252.3 0.7 slice_bitcast_fusion
  253.0 1.5 fusion.42
  254.5 0.6 copy-done.19
  255.0 0.4 copy-done.23
  255.5 1.4 fusion.44
  256.9 0.3 copy-done.26
  257.2 2.6 fusion.30
  (32 shorter events, 0.1 us)
Async XLA Ops:
  0.6 11.8 %copy-start = (bf16[1,1024,768]{2,1,0:T(8,128)(2,1)S(1)}, bf16[1,1024,768]{2,1,0:T(8,128)(2,1)}, u32[]{:S(2)}) copy-start(bf16[1,1024,768]{2,1,0:T(8,128)(2,1)} %param.7) | copy-start | bytes 4718596
  0.6 2.8 %copy-start.21 = (bf16[1,1024,768]{2,1,0:T(8,128)(2,1)S(1)}, bf16[1,1024,768]{2,1,0:T(8,128)(2,1)}, u32[]{:S(2)}) copy-start(bf16[1,1024,768]{2,1,0:T(8,128)(2,1)} %param.13) | copy-start | bytes 4718596
  3.4 2.8 %copy-start.12 = (bf16[4,256,256]{2,1,0:T(8,128)(2,1)S(1)}, bf16[4,256,256]{2,1,0:T(8,128)(2,1)}, u32[]{:S(2)}) copy-start(bf16[4,256,256]{2,1,0:T(8,128)(2,1)} %param.9) | copy-start | bytes 1572868
  6.2 1.1 copy-start.20
  12.4 3.1 %copy-start.22 = (bf16[768,768]{1,0:T(8,128)(2,1)S(1)}, bf16[768,768]{1,0:T(8,128)(2,1)}, u32[]{:S(2)}) copy-start(bf16[768,768]{1,0:T(8,128)(2,1)} %param.10) | copy-start | bytes 3538948
  15.5 3.1 %copy-start.5 = (f32[1024,768]{1,0:T(8,128)}, f32[1024,768]{1,0:T(8,128)S(1)}, u32[]{:S(2)}) copy-start(f32[1024,768]{1,0:T(8,128)S(1)} %add_divide_fusion) | copy-start | bytes 9437188
  15.5 3.1 %copy-start.14 = (bf16[4,256,256]{2,1,0:T(8,128)(2,1)S(1)}, bf16[4,256,256]{2,1,0:T(8,128)(2,1)}, u32[]{:S(2)}) copy-start(bf16[4,256,256]{2,1,0:T(8,128)(2,1)} %param.8) | copy-start | bytes 1572868
  18.7 1.2 copy-start.10
  25.9 1.4 copy-start.1
  104.3 1.2 copy-start.2
  105.5 1.1 copy-start.4
  114.2 2.9 %copy-start.13 = (bf16[4,256,256]{2,1,0:T(8,128)(2,1)S(1)}, bf16[4,256,256]{2,1,0:T(8,128)(2,1)}, u32[]{:S(2)}) copy-start(bf16[4,256,256]{2,1,0:T(8,128)(2,1)} %param.9) | copy-start | bytes 1572868
  118.8 2.7 %copy-start.8 = (bf16[4,768,256]{1,2,0:T(8,128)(2,1)S(1)}, bf16[4,768,256]{1,2,0:T(8,128)(2,1)}, u32[]{:S(2)}) copy-start(bf16[4,768,256]{1,2,0:T(8,128)(2,1)} %convolution_convert_fusion) | copy-start | bytes 4718596
  128.9 5.1 %copy-start.3 = (bf16[64,16,768]{2,1,0:T(8,128)(2,1)S(1)}, bf16[64,16,768]{2,1,0:T(8,128)(2,1)}, u32[]{:S(2)}) copy-start(bf16[64,16,768]{2,1,0:T(8,128)(2,1)} %copy-done.2) | copy-start | bytes 4718596
  138.6 2.7 %copy-start.25 = (bf16[4,256,256]{2,1,0:T(8,128)(2,1)S(1)}, bf16[4,256,256]{2,1,0:T(8,128)(2,1)}, u32[]{:S(2)}) copy-start(bf16[4,256,256]{2,1,0:T(8,128)(2,1)} %convolution_convert_fusion.5) | copy-start | bytes 1572868
  138.7 2.8 %copy-start.9 = (bf16[4,256,768]{2,1,0:T(8,128)(2,1)S(1)}, bf16[4,256,768]{2,1,0:T(8,128)(2,1)}, u32[]{:S(2)}) copy-start(bf16[4,256,768]{2,1,0:T(8,128)(2,1)} %reshape.93) | copy-start | bytes 4718596
  141.3 1.0 copy-start.15
  141.3 2.0 copy-start.7
  142.3 2.2 copy-start.6
  146.5 1.2 copy-start.16
  156.1 2.6 %copy-start.18 = (bf16[1024,768]{1,0:T(8,128)(2,1)S(1)}, bf16[1024,768]{1,0:T(8,128)(2,1)}, u32[]{:S(2)}) copy-start(bf16[1024,768]{1,0:T(8,128)(2,1)} %get-tuple-element.16) | copy-start | bytes 4718596
  167.2 1.6 copy-start.11
  167.2 2.0 copy-start.24
  253.0 2.1 copy-start.19
  253.0 2.5 copy-start.23
  255.5 1.4 copy-start.17
  255.5 1.7 copy-start.26

commit v2 on v0

v2 whole, which is shorter than its diff:
```python
import functools

import jax
import jax.numpy as jnp
from jax import lax
from jax.experimental import pallas as pl
from jax.experimental.pallas import tpu as pltpu
from jax.sharding import PartitionSpec as P

MESH = pl.DeviceIdType.MESH
BF16 = jnp.bfloat16
F32 = jnp.float32
NZ, NX = 4, 16


def dot(left, right):
    return jnp.dot(left, right, preferred_element_type=F32)


def dot_cols(left, right):
    return lax.dot_general(left, right, (((1,), (1,)), ((), ())), preferred_element_type=F32)


def each(count, body):
    def step(i, carry):
        body(i)
        return carry

    lax.fori_loop(0, count, step, 0)


def mega(nz, nx, *refs):
    ns = nz * nx
    rows = 4 * ns
    width = 12 * ns
    half = width // 2
    lanes = half // 3
    (tok_h, ff_h, sf_h, vw_h, gw_h, ow_h, cot_h), refs = refs[:7], refs[7:]
    (res_h, grad_h, first_out, second_out, w_out), refs = refs[:5], refs[5:]
    (tok, ff, sf, vw, gw, ow, cot, tok_t, ff_t, sf_t), refs = refs[:10], refs[10:]
    (bs, bsend, brecv, fsend, frecv, val, sig, mix), refs = refs[:8], refs[8:]
    (tmp, got, dval, dgate, sec, sec_t, res, grad), refs = refs[:8], refs[8:]
    (first, second, term, wide), refs = refs[:4], refs[4:]
    jobs = [refs[7 * n : 7 * n + 7] for n in range(4)]
    refs = refs[28:]
    facs = [refs[5 * n : 5 * n + 5] for n in range(2)]
    refs = refs[10:]
    load_sem, store_sem, a2a_send, a2a_recv, job_send, job_recv, fac_send, fac_recv = refs
    a2a, job, fac = (a2a_send, a2a_recv), (job_send, job_recv), (fac_send, fac_recv)

    dp, seq = lax.axis_index("dp"), lax.axis_index("seq")
    zl, core = dp // 2, lax.rem(dp, 2)
    zh, xy = seq // nx, lax.rem(seq, nx)
    z = zh * 2 + zl
    other = 1 - core
    partner = (zl * 2 + other, seq)
    neighbour = ((1 - zl) * 2 + core, seq)

    loads = [
        pltpu.make_async_copy(src, dst, load_sem.at[i])
        for i, (src, dst) in enumerate(
            ((cot_h, cot), (ow_h, ow), (sf_h, sf), (tok_h, tok), (vw_h, vw), (gw_h, gw), (ff_h, ff))
        )
    ]
    for load in loads:
        load.start()

    barrier = pltpu.get_barrier_semaphore()

    def peer(step):
        return lax.rem(seq + step, ns)

    def greet(i):
        pl.semaphore_signal(barrier, inc=1, device_id=(dp, peer(i + 1)), device_id_type=MESH)

    def greet_column(i):
        device = ((1 - zl) * 2 + core, i * nx + xy)
        pl.semaphore_signal(barrier, inc=1, device_id=device, device_id_type=MESH)

    each(ns - 1, greet)
    each(nz, greet_column)
    pl.semaphore_signal(barrier, inc=1, device_id=partner, device_id_type=MESH)

    def remote(src, dst, sems, k, device):
        return pltpu.make_async_remote_copy(
            src_ref=src,
            dst_ref=dst,
            send_sem=sems[0].at[k],
            recv_sem=sems[1].at[k],
            device_id=device,
            device_id_type=MESH,
        )

    def send_all(src, dst, k):
        def send(i):
            to = peer(i + 1)
            remote(src.at[to], dst.at[seq], a2a, k, (dp, to)).start()

        each(ns - 1, send)
        dst[seq] = src[seq]

    def all_of(src, dst, k):
        return remote(src.at[pl.ds(0, ns - 1)], dst.at[pl.ds(0, ns - 1)], a2a, k, (dp, peer(1)))

    def to_messages(dst):
        tiles = min(8, rows // 8)
        mask = lax.broadcasted_iota(jnp.int32, (tiles, 8, half), 1) < 4

        def block(i):
            at = pl.ds(pl.multiple_of(i * tiles * 8, 8), tiles * 8)
            r = [tmp[k, at, :].reshape(tiles, 8, half) for k in range(4)]
            turned = [pltpu.roll(x, 4, 1) for x in r]
            low = [jnp.where(mask, r[k], turned[k + 1]) for k in (0, 2)]
            high = [jnp.where(mask, turned[k], r[k + 1]) for k in (0, 2)]
            low = jnp.concatenate(low, axis=1).astype(BF16)
            high = jnp.concatenate(high, axis=1).astype(BF16)
            for t in range(tiles):
                dst[(i * tiles + t) * 2] = low[t]
                dst[(i * tiles + t) * 2 + 1] = high[t]

        each(rows // (tiles * 8), block)

    def from_messages(src):
        for j in range(3):
            cols = slice(j * lanes, (j + 1) * lanes)

            def widen(i, j=j, cols=cols):
                at = pl.ds(pl.multiple_of(i * 64, 64), 64)
                part = src[pl.ds(i * 4, 4), :, cols]
                term[j, at, :] = part.reshape(64, lanes).astype(F32)

            each(4 * rows // 64, widen)
            for k in range(4):
                got[k, :, cols] = term[j, pl.ds(k, rows, stride=4), :].astype(BF16)

    def zone(n):
        count = nz if n < 2 else nz // 2
        base = 0 if n < 2 else (n - 2) * count
        member = (zh >= base) & (zh < base + count)
        return count, base, member

    def put_rows(n, which):
        own = jobs[n][0]

        def two(m):
            x = wide[pl.ds(pl.multiple_of(24 * m, 8), 32), :]
            for k in range(2):
                s = 2 * m + k
                block = x[12 * k : 12 * k + 16].astype(BF16)
                own[which, lax.rem(s, nx), s // nx] = block

        each(zone(n)[0] * nx // 2, two)

    def pair_copy(n):
        return remote(jobs[n][0].at[other], jobs[n][1], job, 4 * n, partner)

    def pair_add(n):
        own, pair, u, plane = jobs[n][:4]
        pair_copy(n).wait()

        def add(i):
            u[i] = (own[core, i].astype(F32) + pair[i].astype(F32)).astype(BF16)

        each(nx, add)

        def send(i):
            to = lax.rem(xy + i + 1, nx)
            remote(u.at[to], plane.at[xy], job, 4 * n + 1, (dp, zh * nx + to)).start()

        each(nx - 1, send)
        plane[xy] = u[xy]

    def plane_add(n):
        u, plane, total, col = jobs[n][2:6]
        count, base, member = zone(n)
        remote(
            u.at[pl.ds(0, nx - 1)], plane.at[pl.ds(0, nx - 1)], job, 4 * n + 1, partner
        ).wait()

        def add(q):
            x = plane[0, q].astype(F32)
            for i in range(1, nx):
                x = x + plane[i, q].astype(F32)
            total[q] = x.astype(BF16)

        each(count, add)

        def send(i):
            to_zh, to_zl = base + i // 2, lax.rem(i, 2)

            @pl.when(to_zh * 2 + to_zl != z)
            def _():
                device = (to_zl * 2 + core, to_zh * nx + xy)
                remote(total.at[i // 2], col.at[z], job, 4 * n + 2, device).start()

        each(2 * count, send)

        @pl.when(member)
        def _():
            col[z] = total[zh - base]

    def column_add(n):
        col, fin = jobs[n][5:]
        count, _, member = zone(n)

        def part(size):
            return remote(
                col.at[pl.ds(0, size)], col.at[pl.ds(0, size)], job, 4 * n + 2, partner
            )

        @pl.when(member)
        def _():
            part(2 * nz - 1).wait_recv()
            x = col[0].astype(F32)
            for i in range(1, 2 * nz):
                x = x + col[i].astype(F32)
            fin[core] = x.astype(BF16)
            remote(fin.at[core], fin.at[core], job, 4 * n + 3, partner).start()
            part(2 * count - 1).wait_send()

        @pl.when(jnp.logical_not(member))
        def _():
            part(2 * count).wait_send()

    def finish(n):
        fin = jobs[n][6]

        @pl.when(zone(n)[2])
        def _():
            remote(fin.at[core], fin.at[core], job, 4 * n + 3, partner).wait()
            at = [
                ((0, slice(0, half)), (1, slice(0, half))),
                ((0, slice(half, width)), (1, slice(half, width))),
                ((2, slice(0, half)), (2, slice(half, width))),
                ((2, slice(0, half)), (2, slice(half, width))),
            ][n]
            for k in range(2):
                w_out[at[k][0], :, at[k][1]] = fin[k].astype(F32)

    def factor_start(n, source):
        own, pair = facs[n][:2]
        for k in range(4):
            own[k // 2, k % 2] = source[k].astype(BF16)
        remote(own.at[other], pair, fac, 3 * n, partner).start()

    def factor_pair(n):
        own, pair, u, near = facs[n][:4]
        remote(own.at[other], pair, fac, 3 * n, partner).wait()

        def add(k):
            u[k] = (own[core, k].astype(F32) + pair[k].astype(F32)).astype(BF16)

        each(2, add)
        remote(u, near, fac, 3 * n + 1, neighbour).start()

    def factor_near(n):
        _, _, u, near, fin = facs[n]
        remote(u, near, fac, 3 * n + 1, neighbour).wait()

        def add(k):
            fin[core, k] = (u[k].astype(F32) + near[k].astype(F32)).astype(BF16)

        each(2, add)
        remote(fin.at[core], fin.at[core], fac, 3 * n + 2, partner).start()

    def factor_end(n, store):
        fin = facs[n][4]
        remote(fin.at[core], fin.at[core], fac, 3 * n + 2, partner).wait()
        store.start()

    stores = [
        pltpu.make_async_copy(src, dst, store_sem.at[i])
        for i, (src, dst) in enumerate(
            (
                (res, res_h),
                (grad, grad_h),
                (facs[0][4], first_out),
                (facs[1][4], second_out),
            )
        )
    ]

    wide[width:, :] = jnp.zeros((8, half), F32)

    for load in loads[:3]:
        load.wait()
    for k in range(4):
        sf_t[k] = sf[k].T
    for c in range(2):

        def back(p, c=c):
            part = dot_cols(cot[p], ow[c * half : (c + 1) * half, :]).astype(BF16)
            bs[c, p] = part
            tmp[p] = dot(sf_t[p], part)

        each(4, back)
        to_messages(bsend.at[c])
        if c == 0:
            pl.semaphore_wait(barrier, ns + nz)
        send_all(bsend.at[c], brecv.at[c], c)

    for load in loads[3:]:
        load.wait()
    for c in range(2):
        cols = slice(c * half, (c + 1) * half)

        def forward(a, c=c, cols=cols):
            v = dot(tok[a], vw[:, cols])
            s = jax.nn.sigmoid(dot(tok[a], gw[:, cols]))
            m = (v * s).astype(BF16)
            val[c, a] = v
            sig[c, a] = s
            mix[c, a] = m
            tmp[a] = dot(ff[a], m)

        each(4, forward)
        to_messages(fsend.at[c])
    for k in range(4):
        ff_t[k] = ff[k].T
        tok_t[:, k * rows : (k + 1) * rows] = tok[k].T

    for c in range(2):
        all_of(bsend.at[c], brecv.at[c], c).wait_send()
        send_all(fsend.at[c], frecv.at[c], 2 + c)
        all_of(bsend.at[c], brecv.at[c], c).wait_recv()
        from_messages(brecv.at[c])

        def inner(a, c=c):
            g = got[a]
            part = dot(ff_t[a], g)
            s = sig[c, a]
            ps = part * s
            dval[c, a] = ps.astype(BF16)
            dgate[c, a] = (ps * val[c, a] * (1.0 - s)).astype(BF16)
            more = dot_cols(g, mix[c, a])
            if c == 0:
                first[a] = more
            else:
                first[a] = first[a] + more

        each(4, inner)
        for which, source in enumerate((dval, dgate)):

            def terms(m, c=c, source=source):
                at = pl.ds(pl.multiple_of(m * rows, 8), rows)
                wide[at, :] = dot(tok_t[at, :], source[c].reshape(4 * rows, half))

            each(3, terms)
            put_rows(c, which)
        pair_copy(c).start()
    factor_start(0, first)
    pair_add(0)
    pair_add(1)
    factor_pair(0)

    def grads(a):
        x = dot_cols(dval[0, a], vw[:, :half]) + dot_cols(dval[1, a], vw[:, half:])
        y = dot_cols(dgate[0, a], gw[:, :half]) + dot_cols(dgate[1, a], gw[:, half:])
        grad[a] = (x + y).astype(BF16)

    each(4, grads)
    stores[1].start()

    def second_half(c):
        all_of(fsend.at[c], frecv.at[c], 2 + c).wait()
        from_messages(frecv.at[c])

        def inner(p):
            sec[c, p] = dot(sf[p], got[p]).astype(BF16)

        each(4, inner)
        for k in range(4):
            sec_t[:, k * rows : (k + 1) * rows] = sec[c, k].T
        for which in range(2):
            cols = slice(which * half, (which + 1) * half)
            wide[:half, :] = dot(sec_t[...], cot[:, :, cols].reshape(4 * rows, half))
            put_rows(2 + c, which)
        pair_copy(2 + c).start()

        def outer(p):
            more = dot_cols(bs[c, p], got[p])
            if c == 0:
                second[p] = more
            else:
                second[p] = second[p] + more

        each(4, outer)

    second_half(0)
    plane_add(0)
    plane_add(1)
    factor_near(0)
    pair_add(2)
    second_half(1)
    factor_start(1, second)
    pair_add(3)
    factor_pair(1)
    column_add(0)
    column_add(1)
    plane_add(2)

    def results(p):
        x = dot(sec[0, p], ow[:half, :]) + dot(sec[1, p], ow[half:, :])
        res[p] = x.astype(BF16)

    each(4, results)
    stores[0].start()
    factor_end(0, stores[2])
    plane_add(3)
    factor_near(1)
    column_add(2)
    column_add(3)
    factor_end(1, stores[3])
    for n in range(4):
        finish(n)
    for store in stores:
        store.wait()


def mega_call(nz, nx, *args):
    ns = nz * nx
    rows = 4 * ns
    width = 12 * ns
    half = width // 2
    vmem, sem = pltpu.VMEM, pltpu.SemaphoreType.DMA
    scratch = [
        vmem((4, rows, width), BF16),
        vmem((4, rows, rows), BF16),
        vmem((4, rows, rows), BF16),
        vmem((width, width), BF16),
        vmem((width, width), BF16),
        vmem((width, width), BF16),
        vmem((4, rows, width), BF16),
        vmem((width, 4 * rows), BF16),
        vmem((4, rows, rows), BF16),
        vmem((4, rows, rows), BF16),
        vmem((2, 4, rows, half), BF16),
        vmem((2, ns, 16, half), BF16),
        vmem((2, ns, 16, half), BF16),
        vmem((2, ns, 16, half), BF16),
        vmem((2, ns, 16, half), BF16),
        vmem((2, 4, rows, half), F32),
        vmem((2, 4, rows, half), F32),
        vmem((2, 4, rows, half), BF16),
        vmem((4, rows, half), F32),
        vmem((4, rows, half), BF16),
        vmem((2, 4, rows, half), BF16),
        vmem((2, 4, rows, half), BF16),
        vmem((2, 4, rows, half), BF16),
        vmem((half, 4 * rows), BF16),
        vmem((4, rows, width), BF16),
        vmem((4, rows, width), BF16),
        vmem((4, rows, rows), F32),
        vmem((4, rows, rows), F32),
        vmem((3, 4 * rows, half // 3), F32),
        vmem((width + 8, half), F32),
    ]
    for n in range(4):
        count = nz if n < 2 else nz // 2
        scratch += [
            vmem((2, nx, count, 16, half), BF16),
            vmem((nx, count, 16, half), BF16),
            vmem((nx, count, 16, half), BF16),
            vmem((nx, count, 16, half), BF16),
            vmem((count, 16, half), BF16),
            vmem((2 * nz, 16, half), BF16),
            vmem((2, 16, half), BF16),
        ]
    for _ in range(2):
        scratch += [
            vmem((2, 2, rows, rows), BF16),
            vmem((2, rows, rows), BF16),
            vmem((2, rows, rows), BF16),
            vmem((2, rows, rows), BF16),
            vmem((2, 2, rows, rows), BF16),
        ]
    scratch += [sem((7,)), sem((4,)), sem((4,)), sem((4,)), sem((16,)), sem((16,)), sem((6,)), sem((6,))]
    anywhere = pl.BlockSpec(memory_space=pl.ANY)
    return pl.pallas_call(
        functools.partial(mega, nz, nx),
        out_shape=(
            jax.ShapeDtypeStruct((4, rows, width), BF16),
            jax.ShapeDtypeStruct((4, rows, width), BF16),
            jax.ShapeDtypeStruct((2, 2, rows, rows), BF16),
            jax.ShapeDtypeStruct((2, 2, rows, rows), BF16),
            jax.ShapeDtypeStruct((3, 16, width), F32),
        ),
        in_specs=[anywhere] * 7,
        out_specs=(anywhere,) * 4 + (pl.BlockSpec(memory_space=vmem),),
        scratch_shapes=scratch,
        compiler_params=pltpu.CompilerParams(
            collective_id=0, has_side_effects=True, vmem_limit_bytes=60 * 2**20
        ),
        cost_estimate=pl.CostEstimate(
            flops=14 * 10**9, bytes_accessed=16 * 10**6, transcendentals=10**6
        ),
        name="mixing",
    )(*args)


def shards(
    nz, nx, tokens, first_factor, second_factor, value_weight, gate_weight, out_weight, cotangent
):
    rows, width = 4 * nz * nx, 12 * nz * nx
    result, grad, first, second, weights = mega_call(
        nz,
        nx,
        tokens.reshape(4, rows, width),
        first_factor,
        second_factor,
        value_weight,
        gate_weight,
        out_weight,
        cotangent.reshape(4, rows, width),
    )
    return (
        result.reshape(1, 4 * rows, width),
        grad.reshape(1, 4 * rows, width),
        first.astype(F32).reshape(4, rows, rows),
        second.astype(F32).reshape(4, rows, rows),
        weights[0, :12],
        weights[1, :12],
        weights[2, :12],
    )


def solution(mesh, nz=NZ, nx=NX):
    return jax.shard_map(
        functools.partial(shards, nz, nx),
        mesh=mesh,
        in_specs=(
            P("dp", "seq", None),
            P("seq", None, None),
            P("seq", None, None),
            P(),
            P(),
            P(),
            P("dp", "seq", None),
        ),
        out_specs=(
            P("dp", "seq", None),
            P("dp", "seq", None),
            P("seq", None, None),
            P("seq", None, None),
            P("seq", None),
            P("seq", None),
            P("seq", None),
        ),
        check_vma=False,
    )
```

time: 667 us -> 121 us (0.18)
  blocking collectives: 494 us -> 0 us
  Pallas kernels: 0 us -> 112 us
  waiting for transfers between devices: 56.9 us -> 0 us
  matrix products: 36.9 us -> 0 us
  starting transfers between devices: 26.3 us -> 0 us
  local copies, waits for them, and re-layouts: 30.4 us -> 4.62 us
  between operations: 14.9 us -> 0.65 us
    unnamed x1 -> x0, blocking collectives: 464 us -> none
    pallas_call x0 -> x1, Pallas kernels: none -> 112 us  [mega_call(): pl.pallas_call(functools.partial(mega, nz, nx), out_shape=(jax.ShapeDtype...]
    all_to_all x2 -> x0, waiting for transfers between devices: 56.9 us -> none  [the longest x1 31.9 us: shards(): lax.all_to_all(back_first, 'seq', split_axis=0, concat_axis=1, tiled=True)]
    dot_general x15 -> x0, matrix products: 36.9 us -> none  [the longest x3 8.82 us: contract_rows(): lax.dot_general(left, right, (((0,), (0,)), ((), ())), preferred_element_...]
    psum x1 -> x0, blocking collectives: 29.6 us -> none  [shards(): lax.psum(shares.astype(jnp.bfloat16), 'dp').astype(jnp.float32)]
    all_to_all x2 -> x0, starting transfers between devices: 26.1 us -> none  [the longest x1 15.1 us: shards(): lax.all_to_all(back_first, 'seq', split_axis=0, concat_axis=1, tiled=True)]
    another operation x1 -> x0, local copies, waits for them, and re-layouts: 11 us -> none  [shards(): stacked = jnp.stack([value_term, gate_term, out_term])]
    all_to_all x4 -> x0, local copies, waits for them, and re-layouts: 8.91 us -> none  [the longest x2 4.48 us: shards(): lax.all_to_all(first_pass, 'seq', split_axis=1, concat_axis=0, tiled=True)]
  transfers between devices with their start and end apart: 3 -> 0, of which waited for: 2 -> 0; matrix products, arithmetic and copies ran while one was open for 3% -> 0% of each run, Pallas kernels for 0% -> 0%
where the time goes in v2:
time: 121 us; the launch traced here: 120 us
  Pallas kernels  112 us (93%)
  local copies, waits for them, and re-layouts  4.62 us (4%)
  other arithmetic  2.82 us (2%)
    pallas_call x1, Pallas kernels, mega_call(): pl.pallas_call(functools.partial(mega, nz, nx), out_shape=(jax.ShapeDtype...  112 us
    unnamed x6, local copies, waits for them, and re-layouts  3.12 us
    reshape x1, other arithmetic, shards(): second.astype(F32).reshape(4, rows, rows)  2.82 us

profile of v2, /device:TPU:1, one launch (start us, length us, event | category | flops | bytes accessed | tf_op | source)
XLA Modules:
  0.0 119.7 jit_solution(6003621093511232136)
XLA Ops:
  0.6 111.6 %mixing.1 = (bf16[4,256,768]{2,1,0:T(8,128)(2,1)}, bf16[4,256,768]{2,1,0:T(8,128)(2,1)}, bf16[2,2,256,256]{3,2,1,0:T(8,128)(2,1)}, bf16[2,2,256,256]{3,2,1,0:T(8,128)(2,1)}, f32[3,16,768]{2,1,0:T(8,128)}) custom-call(bf16[4,256,768]{2,1,0:T(8,128)(2,1)} %bitcast.18, bf16[4,256,256]{2,1,0:T(8,128)(2,1)} %refs_1_.1, bf16[4,256,256]{2,1,0:T(8,128)(2,1)} %refs_2_.1, ...), custom_call_target="tpu_custom_call" | custom-call | flops 14000000000 | bytes 16000000 | tf_op jit(solution)/shard_map/mixing/pallas_call | solution.py:479
  112.2 1.5 %slice_bitcast_fusion = (f32[12,768]{1,0:T(8,128)}, f32[12,768]{1,0:T(8,128)}, f32[12,768]{1,0:T(8,128)}) fusion(f32[3,16,768]{2,1,0:T(8,128)} %get-tuple-element.16), kind=kLoop, calls=%fused_computation.2 | loop fusion | bytes 221184 | tf_op jit(solution)/shard_map/squeeze | solution.py:523
  113.7 0.0 copy-start.1
  113.7 2.8 %bitcast_convert_fusion = (f32[4,256,256]{2,1,0:T(8,128)}, f32[4,256,256]{2,1,0:T(8,128)}) fusion(bf16[2,2,256,256]{3,2,1,0:T(8,128)(2,1)} %get-tuple-element.15, bf16[2,2,256,256]{3,2,1,0:T(8,128)(2,1)} %get-tuple-element.14), kind=kLoop, calls=%fused_computation | loop fusion | flops 524288 | bytes 3145728 | tf_op jit(solution)/shard_map/reshape | solution.py:520
  116.6 0.0 copy-done.1
  116.6 0.0 copy-start
  116.6 1.1 copy.16
  117.7 0.8 copy-done
  118.5 1.1 copy.17
Async XLA Ops:
  113.7 2.8 %copy-start.1 = (bf16[4,256,768]{2,1,0:T(8,128)(2,1)S(1)}, bf16[4,256,768]{2,1,0:T(8,128)(2,1)}, u32[]{:S(2)}) copy-start(bf16[4,256,768]{2,1,0:T(8,128)(2,1)} %get-tuple-element.12) | copy-start | bytes 4718596
  116.6 2.0 %copy-start = (bf16[4,256,768]{2,1,0:T(8,128)(2,1)S(1)}, bf16[4,256,768]{2,1,0:T(8,128)(2,1)}, u32[]{:S(2)}) copy-start(bf16[4,256,768]{2,1,0:T(8,128)(2,1)} %get-tuple-element.13) | copy-start | bytes 4718596

commit v3 on v2

v3 whole, which is shorter than its diff:
```python
import functools

import jax
import jax.numpy as jnp
from jax import lax
from jax.experimental import pallas as pl
from jax.experimental.pallas import tpu as pltpu
from jax.sharding import PartitionSpec as P

MESH = pl.DeviceIdType.MESH
BF16 = jnp.bfloat16
F32 = jnp.float32
NZ, NX = 4, 16


def dot(left, right):
    return jnp.dot(left, right, preferred_element_type=F32)


def dot_cols(left, right):
    return lax.dot_general(left, right, (((1,), (1,)), ((), ())), preferred_element_type=F32)


def each(count, body):
    def step(i, carry):
        body(i)
        return carry

    lax.fori_loop(0, count, step, 0)


def mega(nz, nx, *refs):
    ns = nz * nx
    rows = 4 * ns
    width = 12 * ns
    half = width // 2
    lanes = half // 3
    (tok_h, ff_h, sf_h, vw_h, gw_h, ow_h, cot_h), refs = refs[:7], refs[7:]
    (res_h, grad_h, first_out, second_out, w_out), refs = refs[:5], refs[5:]
    (tok, ff, sf, vw, gw, ow, cot, tok_t, ff_t, sf_t), refs = refs[:10], refs[10:]
    bsend, brecv, fsend, frecv = (refs[3 * i : 3 * i + 3] for i in range(4))
    refs = refs[12:]
    (bs, val, sig, mix), refs = refs[:4], refs[4:]
    (tmp, got, dval, dgate, sec, sec_t, res, grad), refs = refs[:8], refs[8:]
    (first, second, term, wide), refs = refs[:4], refs[4:]
    jobs = [refs[7 * n : 7 * n + 7] for n in range(4)]
    refs = refs[28:]
    facs = [refs[5 * n : 5 * n + 5] for n in range(2)]
    refs = refs[10:]
    load_sem, store_sem, a2a_send, a2a_recv, job_send, job_recv, fac_send, fac_recv = refs
    a2a, job, fac = (a2a_send, a2a_recv), (job_send, job_recv), (fac_send, fac_recv)

    dp, seq = lax.axis_index("dp"), lax.axis_index("seq")
    zl, core = dp // 2, lax.rem(dp, 2)
    zh, xy = seq // nx, lax.rem(seq, nx)
    z = zh * 2 + zl
    other = 1 - core
    partner = (zl * 2 + other, seq)
    neighbour = ((1 - zl) * 2 + core, seq)

    loads = [
        pltpu.make_async_copy(src, dst, load_sem.at[i])
        for i, (src, dst) in enumerate(
            ((sf_h, sf), (cot_h, cot), (ow_h, ow), (tok_h, tok), (vw_h, vw), (gw_h, gw), (ff_h, ff))
        )
    ]
    for load in loads[:3]:
        load.start()

    barrier = pltpu.get_barrier_semaphore()

    far = sorted(range(1, nz), key=lambda dz: abs(dz - nz / 2))

    def greet(device):
        pl.semaphore_signal(barrier, inc=1, device_id=device, device_id_type=MESH)

    def greet_row(i):
        to_xy = lax.rem(xy + i, nx)
        for dz in far:
            greet((dp, lax.rem(zh + dz, nz) * nx + to_xy))

        @pl.when(i > 0)
        def _():
            greet((dp, zh * nx + to_xy))

    def greet_column(i):
        for d in range(1, 4):
            greet((lax.rem(dp + d, 4), i * nx + xy))

    each(nx, greet_row)
    each(nz, greet_column)

    def remote(src, dst, sems, k, device):
        return pltpu.make_async_remote_copy(
            src_ref=src,
            dst_ref=dst,
            send_sem=sems[0].at[k],
            recv_sem=sems[1].at[k],
            device_id=device,
            device_id_type=MESH,
        )

    def send_all(src, dst, k):
        def send(to):
            remote(src.at[to], dst.at[seq], a2a, k, (dp, to)).start()

        def row(i):
            for dz in far:
                send(lax.rem(zh + dz, nz) * nx + lax.rem(xy + i, nx))

        each(nx, row)
        each(nx - 1, lambda i: send(zh * nx + lax.rem(xy + i + 1, nx)))
        dst[seq] = src[seq]

    def all_of(src, dst, k):
        some = pl.ds(0, ns - 1)
        return remote(src.at[some], dst.at[some], a2a, k, (dp, lax.rem(seq + 1, ns)))

    def to_messages(dst, start, size):
        tiles = min(8, rows // 8)
        mask = lax.broadcasted_iota(jnp.int32, (tiles, 8, size), 1) < 4

        def block(i):
            at = pl.ds(pl.multiple_of(i * tiles * 8, 8), tiles * 8)
            r = [tmp[k, at, start : start + size].reshape(tiles, 8, size) for k in range(4)]
            turned = [pltpu.roll(x, 4, 1) for x in r]
            low = [jnp.where(mask, r[k], turned[k + 1]) for k in (0, 2)]
            high = [jnp.where(mask, turned[k], r[k + 1]) for k in (0, 2)]
            low = jnp.concatenate(low, axis=1).astype(BF16)
            high = jnp.concatenate(high, axis=1).astype(BF16)
            for t in range(tiles):
                dst[(i * tiles + t) * 2] = low[t]
                dst[(i * tiles + t) * 2 + 1] = high[t]

        each(rows // (tiles * 8), block)

    def from_messages(src, start, size):
        for j in range(size // lanes):
            cols = slice(j * lanes, (j + 1) * lanes)
            to_cols = slice(start + j * lanes, start + (j + 1) * lanes)

            def widen(i, j=j, cols=cols):
                at = pl.ds(pl.multiple_of(i * 64, 64), 64)
                part = src[pl.ds(i * 4, 4), :, cols]
                term[j, at, :] = part.reshape(64, lanes).astype(F32)

            each(4 * rows // 64, widen)
            for k in range(4):
                got[k, :, to_cols] = term[j, pl.ds(k, rows, stride=4), :].astype(BF16)

    def zone(n):
        count = nz if n < 2 else nz // 2
        base = 0 if n < 2 else (n - 2) * count
        inside = (zh >= base) & (zh < base + count)
        return count, base, inside, inside & (zl == n % 2)

    def put_rows(n, which, first_pair, last_pair):
        own = jobs[n][0]

        def two(i):
            m = first_pair + i
            x = wide[which, pl.ds(pl.multiple_of(24 * m, 8), 32), :]
            for k in range(2):
                s = 2 * m + k
                block = x[12 * k : 12 * k + 16].astype(BF16)
                own[which, lax.rem(s, nx), s // nx] = block

        each(last_pair - first_pair, two)

    def pair_copy(n):
        return remote(jobs[n][0].at[other], jobs[n][1], job, 4 * n, partner)

    def pair_add(n):
        own, pair, u, plane = jobs[n][:4]
        pair_copy(n).wait()

        def add(i):
            u[i] = (own[core, i].astype(F32) + pair[i].astype(F32)).astype(BF16)

        each(nx, add)

        def send(i):
            to = lax.rem(xy + i + 1, nx)
            remote(u.at[to], plane.at[xy], job, 4 * n + 1, (dp, zh * nx + to)).start()

        each(nx - 1, send)
        plane[xy] = u[xy]

    def plane_add(n):
        u, plane, total, col = jobs[n][2:6]
        count, base, inside, member = zone(n)
        remote(
            u.at[pl.ds(0, nx - 1)], plane.at[pl.ds(0, nx - 1)], job, 4 * n + 1, partner
        ).wait()

        def add(q):
            x = plane[0, q].astype(F32)
            for i in range(1, nx):
                x = x + plane[i, q].astype(F32)
            total[q] = x.astype(BF16)

        each(count, add)
        if n < 3:

            def send(i):
                @pl.when((base + i != zh) | (zl != n % 2))
                def _():
                    device = ((n % 2) * 2 + core, (base + i) * nx + xy)
                    remote(total.at[i], col.at[z], job, 4 * n + 2, device).start()

            each(count, send)

            @pl.when(member)
            def _():
                col[z] = total[zh - base]

        else:

            def send(i):
                to_dp = lax.rem(i, 4)

                @pl.when((base + i // 4 != zh) | (to_dp != dp))
                def _():
                    device = (to_dp, (base + i // 4) * nx + xy)
                    slot = col.at[core * 2 * nz + z]
                    remote(total.at[i // 4], slot, job, 4 * n + 2, device).start()

            each(4 * count, send)

            @pl.when(inside)
            def _():
                col[core * 2 * nz + z] = total[zh - base]

    def pieces(n, sem, size):
        some = pl.ds(0, size)
        return remote(jobs[n][5].at[some], jobs[n][5].at[some], job, 4 * n + sem, partner)

    def sum_of(col, start):
        x = col[start].astype(F32)
        for i in range(1, 2 * nz):
            x = x + col[start + i].astype(F32)
        return x

    def column_add(n):
        col, fin = jobs[n][5:]
        count, _, _, member = zone(n)

        @pl.when(member)
        def _():
            pieces(n, 2, 2 * nz - 1).wait_recv()
            fin[core] = sum_of(col, 0).astype(BF16)
            for d in range(1, 4):
                device = (lax.rem(dp + d, 4), seq)
                remote(fin.at[core], fin.at[core], job, 4 * n + 3, device).start()
            pieces(n, 2, count - 1).wait_send()

        @pl.when(jnp.logical_not(member))
        def _():
            pieces(n, 2, count).wait_send()

    def finish(n):
        fin = jobs[n][6]
        _, _, inside, member = zone(n)

        @pl.when(inside)
        def _():
            @pl.when(member)
            def _():
                remote(fin.at[other], fin.at[other], job, 4 * n + 3, partner).wait_recv()
                pieces(n, 3, 3).wait_send()

            @pl.when(jnp.logical_not(member))
            def _():
                remote(fin, fin, job, 4 * n + 3, partner).wait_recv()

            at = [
                ((0, slice(0, half)), (1, slice(0, half))),
                ((0, slice(half, width)), (1, slice(half, width))),
                ((2, slice(0, half)), (2, slice(half, width))),
            ][n]
            for k in range(2):
                w_out[at[k][0], :, at[k][1]] = fin[k].astype(F32)

    def finish_last():
        col = jobs[3][5]
        count, _, inside, _ = zone(3)

        @pl.when(inside)
        def _():
            pieces(3, 2, 4 * nz - 1).wait_recv()
            for k in range(2):
                total = sum_of(col, 2 * nz * k).astype(BF16)
                w_out[2, :, k * half : (k + 1) * half] = total.astype(F32)
            pieces(3, 2, 4 * count - 1).wait_send()

        @pl.when(jnp.logical_not(inside))
        def _():
            pieces(3, 2, 4 * count).wait_send()

    def factor_start(n, source):
        own, pair = facs[n][:2]
        for k in range(4):
            own[k // 2, k % 2] = source[k].astype(BF16)
        remote(own.at[other], pair, fac, 5 * n, partner).start()

    def factor_pair(n):
        own, pair, u = facs[n][:3]
        remote(own.at[other], pair, fac, 5 * n, partner).wait()
        for k in range(2):
            u[k] = (own[core, k].astype(F32) + pair[k].astype(F32)).astype(BF16)

    def near_copy(n, k):
        return remote(facs[n][2].at[k], facs[n][3].at[k], fac, 5 * n + 1 + k, neighbour)

    def fin_copy(n, k):
        fin = facs[n][4]
        return remote(fin.at[core, k], fin.at[core, k], fac, 5 * n + 3 + k, partner)

    def factor_near(n):
        _, _, u, near, fin = facs[n]
        for k in range(2):
            near_copy(n, k).wait()
            fin[core, k] = (u[k].astype(F32) + near[k].astype(F32)).astype(BF16)
            fin_copy(n, k).start()

    def factor_end(n, wide_sum, store):
        fin = facs[n][4]
        for k in range(2):
            fin_copy(n, k).wait()
        for k in range(4):
            wide_sum[k] = fin[k // 2, k % 2].astype(F32)
        store.start()

    stores = [
        pltpu.make_async_copy(src, dst, store_sem.at[i])
        for i, (src, dst) in enumerate(
            ((res, res_h), (grad, grad_h), (first, first_out), (second, second_out))
        )
    ]
    for which in range(2):
        wide[which, width:, :] = jnp.zeros((8, half), F32)

    loads[0].wait()
    for k in range(4):
        sf_t[k] = sf[k].T
    loads[1].wait()
    loads[2].wait()
    for load in loads[3:]:
        load.start()
    back_groups = ((0, 0, lanes), (0, lanes, 2 * lanes), (1, 0, half))
    for g, (c, start, size) in enumerate(back_groups):

        def back(p, c=c, start=start, size=size):
            at = c * half + start
            part = dot_cols(cot[p], ow[at : at + size, :]).astype(BF16)
            bs[c, p, :, start : start + size] = part
            tmp[p, :, :size] = dot(sf_t[p], part)

        each(4, back)
        to_messages(bsend[g], 0, size)
        if g == 0:
            pl.semaphore_wait(barrier, ns - 1 + 3 * nz)
        send_all(bsend[g], brecv[g], g)

    for load in loads[3:]:
        load.wait()
    forward_groups = ((0, 0, half), (1, 0, 2 * lanes), (1, 2 * lanes, lanes))
    for c in range(2):
        cols = slice(c * half, (c + 1) * half)

        def forward(a, c=c, cols=cols):
            v = dot(tok[a], vw[:, cols])
            s = jax.nn.sigmoid(dot(tok[a], gw[:, cols]))
            m = (v * s).astype(BF16)
            val[c, a] = v
            sig[c, a] = s
            mix[c, a] = m
            tmp[a] = dot(ff[a], m)

        each(4, forward)
        for g, (group_c, start, size) in enumerate(forward_groups):
            if group_c == c:
                to_messages(fsend[g], start, size)
    for k in range(4):
        ff_t[k] = ff[k].T
        tok_t[:, k * rows : (k + 1) * rows] = tok[k].T

    def back_copy(g):
        return all_of(bsend[g], brecv[g], g)

    def forward_copy(g):
        return all_of(fsend[g], frecv[g], 3 + g)

    for c in range(2):
        groups = [g for g in range(3) if back_groups[g][0] == c]
        for g in groups:
            back_copy(g).wait_send()
        for g in range(3):
            if forward_groups[g][0] == c:
                send_all(fsend[g], frecv[g], 3 + g)
        for g in groups:
            back_copy(g).wait_recv()
            from_messages(brecv[g], *back_groups[g][1:])

        def inner(a, c=c):
            g = got[a]
            part = dot(ff_t[a], g)
            s = sig[c, a]
            ps = part * s
            dval[c, a] = ps.astype(BF16)
            dgate[c, a] = (ps * val[c, a] * (1.0 - s)).astype(BF16)
            more = dot_cols(g, mix[c, a])
            if c == 0:
                first[a] = more
            else:
                first[a] = first[a] + more

        each(4, inner)
        for which, source in enumerate((dval, dgate)):

            def terms(m, c=c, which=which, source=source):
                at = pl.ds(pl.multiple_of(m * rows, 8), rows)
                wide[which, at, :] = dot(tok_t[at, :], source[c].reshape(4 * rows, half))

            each(3, terms)
            put_rows(c, which, 0, ns // 2)
        pair_copy(c).start()
    factor_start(0, first)
    pair_add(0)
    pair_add(1)
    factor_pair(0)
    near_copy(0, 0).start()

    def grads(a):
        x = dot_cols(dval[0, a], vw[:, :half]) + dot_cols(dval[1, a], vw[:, half:])
        y = dot_cols(dgate[0, a], gw[:, :half]) + dot_cols(dgate[1, a], gw[:, half:])
        grad[a] = (x + y).astype(BF16)

    each(4, grads)
    stores[1].start()

    def mix_second(g):
        c, start, size = forward_groups[g]
        cols = slice(start, start + size)
        forward_copy(g).wait_recv()
        from_messages(frecv[g], start, size)

        def inner(p):
            sec[c, p, :, cols] = dot(sf[p], got[p, :, cols]).astype(BF16)

        each(4, inner)
        for k in range(4):
            sec_t[cols, k * rows : (k + 1) * rows] = sec[c, k, :, cols].T
        for which in range(2):
            right = cot[:, :, which * half : (which + 1) * half].reshape(4 * rows, half)
            wide[which, cols, :] = dot(sec_t[cols, :], right)

    def grow_second(g):
        c, start, size = forward_groups[g]
        cols = slice(start, start + size)

        def outer(p):
            more = dot_cols(bs[c, p, :, cols], got[p, :, cols])
            if g == 0:
                second[p] = more
            else:
                second[p] = second[p] + more

        each(4, outer)

    early = 2 * lanes // 24
    mix_second(0)
    for which in range(2):
        put_rows(2, which, 0, ns // 4)
    pair_copy(2).start()
    grow_second(0)
    plane_add(0)
    plane_add(1)
    pair_add(2)
    mix_second(1)
    for which in range(2):
        put_rows(3, which, 0, early)
    grow_second(1)
    for g in range(3):
        forward_copy(g).wait_send()
    near_copy(0, 1).start()
    mix_second(2)
    for which in range(2):
        put_rows(3, which, early, ns // 4)
    pair_copy(3).start()
    grow_second(2)
    factor_start(1, second)
    pair_add(3)
    factor_pair(1)
    for k in range(2):
        near_copy(1, k).start()
    column_add(0)
    column_add(1)
    plane_add(2)
    factor_near(0)

    def results(p):
        x = dot(sec[0, p], ow[:half, :]) + dot(sec[1, p], ow[half:, :])
        res[p] = x.astype(BF16)

    each(4, results)
    stores[0].start()
    plane_add(3)
    factor_end(0, first, stores[2])
    column_add(2)
    for n in range(2):
        finish(n)
    factor_near(1)
    finish(2)
    finish_last()
    factor_end(1, second, stores[3])
    for store in stores:
        store.wait()


def mega_call(nz, nx, *args):
    ns = nz * nx
    rows = 4 * ns
    width = 12 * ns
    half = width // 2
    vmem, sem = pltpu.VMEM, pltpu.SemaphoreType.DMA
    scratch = [
        vmem((4, rows, width), BF16),
        vmem((4, rows, rows), BF16),
        vmem((4, rows, rows), BF16),
        vmem((width, width), BF16),
        vmem((width, width), BF16),
        vmem((width, width), BF16),
        vmem((4, rows, width), BF16),
        vmem((width, 4 * rows), BF16),
        vmem((4, rows, rows), BF16),
        vmem((4, rows, rows), BF16),
    ]
    for sizes in ((1, 2, 3), (1, 2, 3), (3, 2, 1), (3, 2, 1)):
        scratch += [vmem((ns, 16, half // 3 * size), BF16) for size in sizes]
    scratch += [
        vmem((2, 4, rows, half), BF16),
        vmem((2, 4, rows, half), F32),
        vmem((2, 4, rows, half), F32),
        vmem((2, 4, rows, half), BF16),
        vmem((4, rows, half), F32),
        vmem((4, rows, half), BF16),
        vmem((2, 4, rows, half), BF16),
        vmem((2, 4, rows, half), BF16),
        vmem((2, 4, rows, half), BF16),
        vmem((half, 4 * rows), BF16),
        vmem((4, rows, width), BF16),
        vmem((4, rows, width), BF16),
        vmem((4, rows, rows), F32),
        vmem((4, rows, rows), F32),
        vmem((3, 4 * rows, half // 3), F32),
        vmem((2, width + 8, half), F32),
    ]
    for n in range(4):
        count = nz if n < 2 else nz // 2
        scratch += [
            vmem((2, nx, count, 16, half), BF16),
            vmem((nx, count, 16, half), BF16),
            vmem((nx, count, 16, half), BF16),
            vmem((nx, count, 16, half), BF16),
            vmem((count, 16, half), BF16),
            vmem((4 * nz if n == 3 else 2 * nz, 16, half), BF16),
            vmem((2, 16, half), BF16),
        ]
    for _ in range(2):
        scratch += [
            vmem((2, 2, rows, rows), BF16),
            vmem((2, rows, rows), BF16),
            vmem((2, rows, rows), BF16),
            vmem((2, rows, rows), BF16),
            vmem((2, 2, rows, rows), BF16),
        ]
    scratch += [sem((count,)) for count in (7, 4, 6, 6, 16, 16, 10, 10)]
    anywhere = pl.BlockSpec(memory_space=pl.ANY)
    return pl.pallas_call(
        functools.partial(mega, nz, nx),
        out_shape=(
            jax.ShapeDtypeStruct((4, rows, width), BF16),
            jax.ShapeDtypeStruct((4, rows, width), BF16),
            jax.ShapeDtypeStruct((4, rows, rows), F32),
            jax.ShapeDtypeStruct((4, rows, rows), F32),
            jax.ShapeDtypeStruct((3, 16, width), F32),
        ),
        in_specs=[anywhere] * 7,
        out_specs=(anywhere,) * 4 + (pl.BlockSpec(memory_space=vmem),),
        scratch_shapes=scratch,
        compiler_params=pltpu.CompilerParams(
            collective_id=0, has_side_effects=True, vmem_limit_bytes=60 * 2**20
        ),
        cost_estimate=pl.CostEstimate(
            flops=14 * 10**9, bytes_accessed=16 * 10**6, transcendentals=10**6
        ),
        name="mixing",
    )(*args)


def deliver(*refs):
    sources, weights, targets, parts, sem = refs[:4], refs[4], refs[5:9], refs[9:12], refs[12]
    copies = [
        pltpu.make_async_copy(src.at[i], dst.at[i], sem.at[4 * n + i])
        for n, (src, dst) in enumerate(zip(sources, targets))
        for i in range(4)
    ]
    for copy in copies:
        copy.start()
    for i in range(3):
        parts[i][...] = weights[i, :12, :]
    for copy in copies:
        copy.wait()


def deliver_call(*arrays):
    anywhere, vmem = pl.BlockSpec(memory_space=pl.ANY), pl.BlockSpec(memory_space=pltpu.VMEM)
    small = jax.ShapeDtypeStruct((12, arrays[4].shape[2]), F32)
    return pl.pallas_call(
        deliver,
        out_shape=tuple(jax.ShapeDtypeStruct(x.shape, x.dtype) for x in arrays[:4]) + (small,) * 3,
        in_specs=[anywhere] * 4 + [vmem],
        out_specs=(anywhere,) * 4 + (vmem,) * 3,
        scratch_shapes=[pltpu.SemaphoreType.DMA((16,))],
        name="deliver",
    )(*arrays)


def shards(
    nz, nx, tokens, first_factor, second_factor, value_weight, gate_weight, out_weight, cotangent
):
    rows, width = 4 * nz * nx, 12 * nz * nx
    arrays = mega_call(
        nz,
        nx,
        tokens.reshape(4, rows, width),
        first_factor,
        second_factor,
        value_weight,
        gate_weight,
        out_weight,
        cotangent.reshape(4, rows, width),
    )
    result, grad, first, second, value_sum, gate_sum, out_sum = deliver_call(*arrays)
    return (
        result.reshape(1, 4 * rows, width),
        grad.reshape(1, 4 * rows, width),
        first,
        second,
        value_sum,
        gate_sum,
        out_sum,
    )


def solution(mesh, nz=NZ, nx=NX):
    return jax.shard_map(
        functools.partial(shards, nz, nx),
        mesh=mesh,
        in_specs=(
            P("dp", "seq", None),
            P("seq", None, None),
            P("seq", None, None),
            P(),
            P(),
            P(),
            P("dp", "seq", None),
        ),
        out_specs=(
            P("dp", "seq", None),
            P("dp", "seq", None),
            P("seq", None, None),
            P("seq", None, None),
            P("seq", None),
            P("seq", None),
            P("seq", None),
        ),
        check_vma=False,
    )
```

time: 121 us -> 274 us (2.26)
  Pallas kernels: 112 us -> 270 us
  local copies, waits for them, and re-layouts: 4.62 us -> 0 us
  other arithmetic: 2.82 us -> 0 us
    pallas_call x0 -> x1, Pallas kernels: none -> 162 us  [deliver_call(): pl.pallas_call(deliver, out_shape=tuple((jax.ShapeDtypeStruct(x.shape, x....]
    pallas_call x1, Pallas kernels: 112 us -> 108 us  [mega_call(): pl.pallas_call(functools.partial(mega, nz, nx), out_shape=(jax.ShapeDtype...]
    unnamed x6 -> x0, local copies, waits for them, and re-layouts: 3.12 us -> none
    reshape x1 -> x0, other arithmetic: 2.82 us -> none  [shards(): second.astype(F32).reshape(4, rows, rows)]
where the time goes in v3:
time: 274 us; the launch traced here: 270 us
  Pallas kernels  270 us (99%)
    pallas_call x1, Pallas kernels, deliver_call(): pl.pallas_call(deliver, out_shape=tuple((jax.ShapeDtypeStruct(x.shape, x....  162 us
    pallas_call x1, Pallas kernels, mega_call(): pl.pallas_call(functools.partial(mega, nz, nx), out_shape=(jax.ShapeDtype...  108 us

profile of v3, /device:TPU:1, one launch (start us, length us, event | category | flops | bytes accessed | tf_op | source)
XLA Modules:
  0.0 270.5 jit_solution(15888658333671448102)
XLA Ops:
  0.6 108.2 %mixing.1 = (bf16[4,256,768]{2,1,0:T(8,128)(2,1)}, bf16[4,256,768]{2,1,0:T(8,128)(2,1)}, f32[4,256,256]{2,1,0:T(8,128)}, f32[4,256,256]{2,1,0:T(8,128)}, f32[3,16,768]{2,1,0:T(8,128)}) custom-call(bf16[4,256,768]{2,1,0:T(8,128)(2,1)} %bitcast.4, bf16[4,256,256]{2,1,0:T(8,128)(2,1)} %refs_1_.1, bf16[4,256,256]{2,1,0:T(8,128)(2,1)} %refs_2_.1, ...), custom_call_target="tpu_custom_call" | custom-call | flops 14000000000 | bytes 16000000 | tf_op jit(solution)/shard_map/mixing/pallas_call | solution.py:580
  108.9 161.6 %deliver.1 = (bf16[4,256,768]{2,1,0:T(8,128)(2,1)}, bf16[4,256,768]{2,1,0:T(8,128)(2,1)}, f32[4,256,256]{2,1,0:T(8,128)}, f32[4,256,256]{2,1,0:T(8,128)}, f32[12...) custom-call(bf16[4,256,768]{2,1,0:T(8,128)(2,1)} %get-tuple-element.19.refs_0_, ...), custom_call_target="tpu_custom_call" | custom-call | tf_op jit(solution)/shard_map/deliver/pallas_call | solution.py:620

commit v4 on v3

--- a/solution.py
+++ b/solution.py
@@ -27,6 +27,10 @@
         return carry
 
     lax.fori_loop(0, count, step, 0)
+
+
+def zone_of(nz, n):
+    return ((nz, 0), (nz, 0), (nz // 2, 0), (nz // 4, nz // 2), (nz // 4, 3 * nz // 4))[n]
 
 
 def mega(nz, nx, *refs):
@@ -36,15 +40,15 @@
     half = width // 2
     lanes = half // 3
     (tok_h, ff_h, sf_h, vw_h, gw_h, ow_h, cot_h), refs = refs[:7], refs[7:]
-    (res_h, grad_h, first_out, second_out, w_out), refs = refs[:5], refs[5:]
+    (res_h, grad_h, first_out, second_out), w_out, refs = refs[:4], refs[4:7], refs[7:]
     (tok, ff, sf, vw, gw, ow, cot, tok_t, ff_t, sf_t), refs = refs[:10], refs[10:]
     bsend, brecv, fsend, frecv = (refs[3 * i : 3 * i + 3] for i in range(4))
     refs = refs[12:]
     (bs, val, sig, mix), refs = refs[:4], refs[4:]
     (tmp, got, dval, dgate, sec, sec_t, res, grad), refs = refs[:8], refs[8:]
     (first, second, term, wide), refs = refs[:4], refs[4:]
-    jobs = [refs[7 * n : 7 * n + 7] for n in range(4)]
-    refs = refs[28:]
+    jobs = [refs[7 * n : 7 * n + 7] for n in range(5)]
+    refs = refs[35:]
     facs = [refs[5 * n : 5 * n + 5] for n in range(2)]
     refs = refs[10:]
     load_sem, store_sem, a2a_send, a2a_recv, job_send, job_recv, fac_send, fac_recv = refs
@@ -58,14 +62,18 @@
     partner = (zl * 2 + other, seq)
     neighbour = ((1 - zl) * 2 + core, seq)
 
+    back_groups = ((0, 0, lanes), (0, lanes, 2 * lanes), (1, 0, half))
+    parts = [(sf_h, sf)]
+    for c, start, size in back_groups:
+        at = pl.ds(c * half + start, size)
+        parts.append((ow_h.at[at, :], ow.at[at, :]))
+    parts += [(cot_h.at[p], cot.at[p]) for p in range(4)]
+    parts += [(tok_h, tok), (vw_h, vw), (gw_h, gw), (ff_h, ff)]
     loads = [
-        pltpu.make_async_copy(src, dst, load_sem.at[i])
-        for i, (src, dst) in enumerate(
-            ((sf_h, sf), (cot_h, cot), (ow_h, ow), (tok_h, tok), (vw_h, vw), (gw_h, gw), (ff_h, ff))
-        )
+        pltpu.make_async_copy(src, dst, load_sem.at[i]) for i, (src, dst) in enumerate(parts)
     ]
-    for load in loads[:3]:
-        load.start()
+    for i in (0, 1, 4, 5, 6, 7, 2, 3):
+        loads[i].start()
 
     barrier = pltpu.get_barrier_semaphore()
 
@@ -149,23 +157,22 @@
                 got[k, :, to_cols] = term[j, pl.ds(k, rows, stride=4), :].astype(BF16)
 
     def zone(n):
-        count = nz if n < 2 else nz // 2
-        base = 0 if n < 2 else (n - 2) * count
+        count, base = zone_of(nz, n)
         inside = (zh >= base) & (zh < base + count)
         return count, base, inside, inside & (zl == n % 2)
 
-    def put_rows(n, which, first_pair, last_pair):
+    def put_rows(n, which, start, stop, offset=0):
         own = jobs[n][0]
 
         def two(i):
-            m = first_pair + i
-            x = wide[which, pl.ds(pl.multiple_of(24 * m, 8), 32), :]
+            m = start + i
+            x = wide[which, pl.ds(pl.multiple_of(24 * (m + offset), 8), 32), :]
             for k in range(2):
                 s = 2 * m + k
                 block = x[12 * k : 12 * k + 16].astype(BF16)
                 own[which, lax.rem(s, nx), s // nx] = block
 
-        each(last_pair - first_pair, two)
+        each(stop - start, two)
 
     def pair_copy(n):
         return remote(jobs[n][0].at[other], jobs[n][1], job, 4 * n, partner)
@@ -279,42 +286,49 @@
                 ((2, slice(0, half)), (2, slice(half, width))),
             ][n]
             for k in range(2):
-                w_out[at[k][0], :, at[k][1]] = fin[k].astype(F32)
-
-    def finish_last():
-        col = jobs[3][5]
-        count, _, inside, _ = zone(3)
+                w_out[at[k][0]][:, at[k][1]] = fin[k].astype(F32)[:12]
+
+    def finish_last(n):
+        col = jobs[n][5]
+        count, _, inside, _ = zone(n)
 
         @pl.when(inside)
         def _():
-            pieces(3, 2, 4 * nz - 1).wait_recv()
+            pieces(n, 2, 4 * nz - 1).wait_recv()
             for k in range(2):
                 total = sum_of(col, 2 * nz * k).astype(BF16)
-                w_out[2, :, k * half : (k + 1) * half] = total.astype(F32)
-            pieces(3, 2, 4 * count - 1).wait_send()
+                w_out[2][:, k * half : (k + 1) * half] = total.astype(F32)[:12]
+            pieces(n, 2, 4 * count - 1).wait_send()
 
         @pl.when(jnp.logical_not(inside))
         def _():
-            pieces(3, 2, 4 * count).wait_send()
+            pieces(n, 2, 4 * count).wait_send()
+
+    def factor_copy(n, k):
+        own, pair = facs[n][:2]
+        return remote(own.at[other, k], pair.at[k], fac, 6 * n + k, partner)
 
     def factor_start(n, source):
-        own, pair = facs[n][:2]
-        for k in range(4):
-            own[k // 2, k % 2] = source[k].astype(BF16)
-        remote(own.at[other], pair, fac, 5 * n, partner).start()
-
-    def factor_pair(n):
+        own = facs[n][0]
+        for k in range(2):
+            for h in range(2):
+                own[h, k] = source[2 * h + k].astype(BF16)
+            factor_copy(n, k).start()
+
+    def factor_pair(n, send):
         own, pair, u = facs[n][:3]
-        remote(own.at[other], pair, fac, 5 * n, partner).wait()
         for k in range(2):
+            factor_copy(n, k).wait()
             u[k] = (own[core, k].astype(F32) + pair[k].astype(F32)).astype(BF16)
+            if k < send:
+                near_copy(n, k).start()
 
     def near_copy(n, k):
-        return remote(facs[n][2].at[k], facs[n][3].at[k], fac, 5 * n + 1 + k, neighbour)
+        return remote(facs[n][2].at[k], facs[n][3].at[k], fac, 6 * n + 2 + k, neighbour)
 
     def fin_copy(n, k):
         fin = facs[n][4]
-        return remote(fin.at[core, k], fin.at[core, k], fac, 5 * n + 3 + k, partner)
+        return remote(fin.at[core, k], fin.at[core, k], fac, 6 * n + 4 + k, partner)
 
     def factor_near(n):
         _, _, u, near, fin = facs[n]
@@ -340,15 +354,8 @@
     for which in range(2):
         wide[which, width:, :] = jnp.zeros((8, half), F32)
 
-    loads[0].wait()
-    for k in range(4):
-        sf_t[k] = sf[k].T
-    loads[1].wait()
-    loads[2].wait()
-    for load in loads[3:]:
-        load.start()
-    back_groups = ((0, 0, lanes), (0, lanes, 2 * lanes), (1, 0, half))
     for g, (c, start, size) in enumerate(back_groups):
+        loads[1 + g].wait()
 
         def back(p, c=c, start=start, size=size):
             at = c * half + start
@@ -356,13 +363,22 @@
             bs[c, p, :, start : start + size] = part
             tmp[p, :, :size] = dot(sf_t[p], part)
 
-        each(4, back)
+        if g == 0:
+            loads[0].wait()
+            for p in range(4):
+                sf_t[p] = sf[p].T
+                loads[4 + p].wait()
+                back(p)
+            for load in loads[8:]:
+                load.start()
+        else:
+            each(4, back)
         to_messages(bsend[g], 0, size)
         if g == 0:
             pl.semaphore_wait(barrier, ns - 1 + 3 * nz)
         send_all(bsend[g], brecv[g], g)
 
-    for load in loads[3:]:
+    for load in loads[8:]:
         load.wait()
     forward_groups = ((0, 0, half), (1, 0, 2 * lanes), (1, 2 * lanes, lanes))
     for c in range(2):
@@ -398,6 +414,8 @@
         for g in range(3):
             if forward_groups[g][0] == c:
                 send_all(fsend[g], frecv[g], 3 + g)
+        if c == 1:
+            pair_add(0)
         for g in groups:
             back_copy(g).wait_recv()
             from_messages(brecv[g], *back_groups[g][1:])
@@ -426,10 +444,8 @@
             put_rows(c, which, 0, ns // 2)
         pair_copy(c).start()
     factor_start(0, first)
-    pair_add(0)
     pair_add(1)
-    factor_pair(0)
-    near_copy(0, 0).start()
+    factor_pair(0, 1)
 
     def grads(a):
         x = dot_cols(dval[0, a], vw[:, :half]) + dot_cols(dval[1, a], vw[:, half:])
@@ -438,6 +454,7 @@
 
     each(4, grads)
     stores[1].start()
+    plane_add(0)
 
     def mix_second(g):
         c, start, size = forward_groups[g]
@@ -468,35 +485,38 @@
 
         each(4, outer)
 
-    early = 2 * lanes // 24
     mix_second(0)
     for which in range(2):
         put_rows(2, which, 0, ns // 4)
     pair_copy(2).start()
     grow_second(0)
-    plane_add(0)
     plane_add(1)
     pair_add(2)
+    pairs = ns // 8
+    early = 2 * lanes // 24 - pairs
     mix_second(1)
     for which in range(2):
-        put_rows(3, which, 0, early)
+        put_rows(3, which, 0, pairs)
+    pair_copy(3).start()
+    for which in range(2):
+        put_rows(4, which, 0, early, pairs)
     grow_second(1)
+    pair_add(3)
     for g in range(3):
         forward_copy(g).wait_send()
     near_copy(0, 1).start()
+    plane_add(2)
+    column_add(0)
+    column_add(1)
     mix_second(2)
     for which in range(2):
-        put_rows(3, which, early, ns // 4)
-    pair_copy(3).start()
+        put_rows(4, which, early, pairs, pairs)
+    pair_copy(4).start()
     grow_second(2)
     factor_start(1, second)
-    pair_add(3)
-    factor_pair(1)
-    for k in range(2):
-        near_copy(1, k).start()
-    column_add(0)
-    column_add(1)
-    plane_add(2)
+    pair_add(4)
+    factor_pair(1, 2)
+    plane_add(3)
     factor_near(0)
 
     def results(p):
@@ -505,14 +525,15 @@
 
     each(4, results)
     stores[0].start()
-    plane_add(3)
     factor_end(0, first, stores[2])
+    plane_add(4)
     column_add(2)
     for n in range(2):
         finish(n)
     factor_near(1)
     finish(2)
-    finish_last()
+    finish_last(3)
+    finish_last(4)
     factor_end(1, second, stores[3])
     for store in stores:
         store.wait()
@@ -556,15 +577,15 @@
         vmem((3, 4 * rows, half // 3), F32),
         vmem((2, width + 8, half), F32),
     ]
-    for n in range(4):
-        count = nz if n < 2 else nz // 2
+    for n in range(5):
+        count, _ = zone_of(nz, n)
         scratch += [
             vmem((2, nx, count, 16, half), BF16),
             vmem((nx, count, 16, half), BF16),
             vmem((nx, count, 16, half), BF16),
             vmem((nx, count, 16, half), BF16),
             vmem((count, 16, half), BF16),
-            vmem((4 * nz if n == 3 else 2 * nz, 16, half), BF16),
+            vmem((4 * nz if n > 2 else 2 * nz, 16, half), BF16),
             vmem((2, 16, half), BF16),
         ]
     for _ in range(2):
@@ -575,7 +596,7 @@
             vmem((2, rows, rows), BF16),
             vmem((2, 2, rows, rows), BF16),
         ]
-    scratch += [sem((count,)) for count in (7, 4, 6, 6, 16, 16, 10, 10)]
+    scratch += [sem((count,)) for count in (12, 4, 6, 6, 20, 20, 12, 12)]
     anywhere = pl.BlockSpec(memory_space=pl.ANY)
     return pl.pallas_call(
         functools.partial(mega, nz, nx),
@@ -584,10 +605,10 @@
             jax.ShapeDtypeStruct((4, rows, width), BF16),
             jax.ShapeDtypeStruct((4, rows, rows), F32),
             jax.ShapeDtypeStruct((4, rows, rows), F32),
-            jax.ShapeDtypeStruct((3, 16, width), F32),
-        ),
+        )
+        + (jax.ShapeDtypeStruct((12, width), F32),) * 3,
         in_specs=[anywhere] * 7,
-        out_specs=(anywhere,) * 4 + (pl.BlockSpec(memory_space=vmem),),
+        out_specs=(anywhere,) * 4 + (pl.BlockSpec(memory_space=vmem),) * 3,
         scratch_shapes=scratch,
         compiler_params=pltpu.CompilerParams(
             collective_id=0, has_side_effects=True, vmem_limit_bytes=60 * 2**20
@@ -599,39 +620,11 @@
     )(*args)
 
 
-def deliver(*refs):
-    sources, weights, targets, parts, sem = refs[:4], refs[4], refs[5:9], refs[9:12], refs[12]
-    copies = [
-        pltpu.make_async_copy(src.at[i], dst.at[i], sem.at[4 * n + i])
-        for n, (src, dst) in enumerate(zip(sources, targets))
-        for i in range(4)
-    ]
-    for copy in copies:
-        copy.start()
-    for i in range(3):
-        parts[i][...] = weights[i, :12, :]
-    for copy in copies:
-        copy.wait()
-
-
-def deliver_call(*arrays):
-    anywhere, vmem = pl.BlockSpec(memory_space=pl.ANY), pl.BlockSpec(memory_space=pltpu.VMEM)
-    small = jax.ShapeDtypeStruct((12, arrays[4].shape[2]), F32)
-    return pl.pallas_call(
-        deliver,
-        out_shape=tuple(jax.ShapeDtypeStruct(x.shape, x.dtype) for x in arrays[:4]) + (small,) * 3,
-        in_specs=[anywhere] * 4 + [vmem],
-        out_specs=(anywhere,) * 4 + (vmem,) * 3,
-        scratch_shapes=[pltpu.SemaphoreType.DMA((16,))],
-        name="deliver",
-    )(*arrays)
-
-
 def shards(
     nz, nx, tokens, first_factor, second_factor, value_weight, gate_weight, out_weight, cotangent
 ):
     rows, width = 4 * nz * nx, 12 * nz * nx
-    arrays = mega_call(
+    result, grad, first, second, value_sum, gate_sum, out_sum = mega_call(
         nz,
         nx,
         tokens.reshape(4, rows, width),
@@ -642,7 +635,6 @@
         out_weight,
         cotangent.reshape(4, rows, width),
     )
-    result, grad, first, second, value_sum, gate_sum, out_sum = deliver_call(*arrays)
     return (
         result.reshape(1, 4 * rows, width),
         grad.reshape(1, 4 * rows, width),

time: 274 us -> 116 us (0.42); the launches traced: 270 us -> 116 us
  Pallas kernels: 270 us -> 106 us
  local copies, waits for them, and re-layouts: 0 us -> 9.01 us
    pallas_call x1 -> x0, Pallas kernels: 162 us -> none  [deliver_call(): pl.pallas_call(deliver, out_shape=tuple((jax.ShapeDtypeStruct(x.shape, x....]
    unnamed x0 -> x19, local copies, waits for them, and re-layouts: none -> 9.01 us
where the time goes in v4:
time: 116 us
  Pallas kernels  106 us (91%)
  local copies, waits for them, and re-layouts  9.01 us (8%)
    pallas_call x1, Pallas kernels, mega_call(): pl.pallas_call(functools.partial(mega, nz, nx), out_shape=(jax.ShapeDtype...  106 us
    unnamed x19, local copies, waits for them, and re-layouts  9.01 us

profile of v4, /device:TPU:1, one launch (start us, length us, event | category | flops | bytes accessed | tf_op | source)
XLA Modules:
  0.0 115.6 jit_solution(2560897206543335205)
XLA Ops:
  0.6 105.9 %mixing.1 = (bf16[4,256,768]{2,1,0:T(8,128)(2,1)}, bf16[4,256,768]{2,1,0:T(8,128)(2,1)}, f32[4,256,256]{2,1,0:T(8,128)}, f32[4,256,256]{2,1,0:T(8,128)}, f32[12,...) custom-call(bf16[4,256,768]{2,1,0:T(8,128)(2,1)} %bitcast.6, bf16[4,256,256]{2,1,0:T(8,128)(2,1)} %refs_1_.1, ...), custom_call_target="tpu_custom_call" | custom-call | flops 14000000000 | bytes 16000000 | tf_op jit(solution)/shard_map/mixing/pallas_call | solution.py:601
  106.6 0.0 copy-start
  106.6 2.8 %copy.21 = bf16[1,1024,768]{2,1,0:T(8,128)(2,1)} copy(bf16[1,1024,768]{2,1,0:T(8,128)(2,1)} %bitcast.5) | data formatting | bytes 3145728
  109.4 0.0 copy-done
  109.4 0.0 copy-start.2
  109.4 1.1 copy.22
  110.5 0.6 copy-done.2
  111.2 0.0 copy-start.1
  111.2 1.0 copy.23
  112.1 0.6 copy-done.1
  112.8 0.0 copy-start.5
  112.8 0.0 copy-start.4
  112.8 0.0 copy-start.3
  112.8 1.0 copy.24
  113.7 0.0 copy-done.5
  113.7 0.6 copy.25
  114.4 0.0 copy-done.4
  114.4 0.6 copy.26
  115.0 0.0 copy-done.3
  115.0 0.6 copy.27
Async XLA Ops:
  106.6 2.8 %copy-start = (bf16[4,256,768]{2,1,0:T(8,128)(2,1)S(1)}, bf16[4,256,768]{2,1,0:T(8,128)(2,1)}, u32[]{:S(2)}) copy-start(bf16[4,256,768]{2,1,0:T(8,128)(2,1)} %get-tuple-element.15) | copy-start | bytes 4718596
  109.4 1.8 %copy-start.2 = (f32[4,256,256]{2,1,0:T(8,128)S(1)}, f32[4,256,256]{2,1,0:T(8,128)}, u32[]{:S(2)}) copy-start(f32[4,256,256]{2,1,0:T(8,128)} %get-tuple-element.30) | copy-start | bytes 3145732
  111.2 1.6 %copy-start.1 = (f32[4,256,256]{2,1,0:T(8,128)S(1)}, f32[4,256,256]{2,1,0:T(8,128)}, u32[]{:S(2)}) copy-start(f32[4,256,256]{2,1,0:T(8,128)} %get-tuple-element.31) | copy-start | bytes 3145732
  112.8 1.0 copy-start.5
  112.8 1.6 %copy-start.4 = (f32[12,768]{1,0:T(8,128)S(1)}, f32[12,768]{1,0:T(8,128)}, u32[]{:S(2)}) copy-start(f32[12,768]{1,0:T(8,128)} %get-tuple-element.33) | copy-start | bytes 110596
  112.8 2.2 %copy-start.3 = (f32[12,768]{1,0:T(8,128)S(1)}, f32[12,768]{1,0:T(8,128)}, u32[]{:S(2)}) copy-start(f32[12,768]{1,0:T(8,128)} %get-tuple-element.34) | copy-start | bytes 110596

commit v5 on v4

--- a/solution.py
+++ b/solution.py
@@ -39,19 +39,19 @@
     width = 12 * ns
     half = width // 2
     lanes = half // 3
+    side = int(nx**0.5)
     (tok_h, ff_h, sf_h, vw_h, gw_h, ow_h, cot_h), refs = refs[:7], refs[7:]
-    (res_h, grad_h, first_out, second_out), w_out, refs = refs[:4], refs[4:7], refs[7:]
+    (res, grad, first, second), w_out, refs = refs[:4], refs[4:7], refs[7:]
     (tok, ff, sf, vw, gw, ow, cot, tok_t, ff_t, sf_t), refs = refs[:10], refs[10:]
     bsend, brecv, fsend, frecv = (refs[3 * i : 3 * i + 3] for i in range(4))
     refs = refs[12:]
     (bs, val, sig, mix), refs = refs[:4], refs[4:]
-    (tmp, got, dval, dgate, sec, sec_t, res, grad), refs = refs[:8], refs[8:]
-    (first, second, term, wide), refs = refs[:4], refs[4:]
+    (tmp, got, dval, dgate, sec, sec_t, term, wide), refs = refs[:8], refs[8:]
     jobs = [refs[7 * n : 7 * n + 7] for n in range(5)]
-    refs = refs[35:]
+    plane_b, refs = refs[35:37], refs[37:]
     facs = [refs[5 * n : 5 * n + 5] for n in range(2)]
     refs = refs[10:]
-    load_sem, store_sem, a2a_send, a2a_recv, job_send, job_recv, fac_send, fac_recv = refs
+    load_sem, a2a_send, a2a_recv, job_send, job_recv, fac_send, fac_recv = refs
     a2a, job, fac = (a2a_send, a2a_recv), (job_send, job_recv), (fac_send, fac_recv)
 
     dp, seq = lax.axis_index("dp"), lax.axis_index("seq")
@@ -170,12 +170,15 @@
             for k in range(2):
                 s = 2 * m + k
                 block = x[12 * k : 12 * k + 16].astype(BF16)
-                own[which, lax.rem(s, nx), s // nx] = block
+                place = lax.rem(s, nx)
+                if n < 2 and which == 1:
+                    place = lax.rem(place, side) * side + place // side
+                own[which, place, s // nx] = block
 
         each(stop - start, two)
 
     def pair_copy(n):
-        return remote(jobs[n][0].at[other], jobs[n][1], job, 4 * n, partner)
+        return remote(jobs[n][0].at[other], jobs[n][1], job, 5 * n, partner)
 
     def pair_add(n):
         own, pair, u, plane = jobs[n][:4]
@@ -185,24 +188,71 @@
             u[i] = (own[core, i].astype(F32) + pair[i].astype(F32)).astype(BF16)
 
         each(nx, add)
+        if n < 2:
+
+            def send_side(i):
+                to = lax.rem(mine + i + 1, side)
+                src, dst = u.at[pl.ds(to * side, side)], plane.at[pl.ds(mine * side, side)]
+                remote(src, dst, job, 5 * n + 1, along(to, crossed)).start()
+
+            each(side - 1, send_side)
+
+            def keep(i):
+                plane[mine * side + i] = u[mine * side + i]
+
+            each(side, keep)
+        else:
+
+            def send(i):
+                to = lax.rem(xy + i + 1, nx)
+                remote(u.at[to], plane.at[xy], job, 5 * n + 1, (dp, zh * nx + to)).start()
+
+            each(nx - 1, send)
+            plane[xy] = u[xy]
+
+    mine = (1 - core) * (xy // side) + core * lax.rem(xy, side)
+    crossed = core * (xy // side) + (1 - core) * lax.rem(xy, side)
+
+    def along(at_mine, at_crossed):
+        place = (1 - core) * (at_mine * side + at_crossed) + core * (at_crossed * side + at_mine)
+        return dp, zh * nx + place
+
+    def side_add(n):
+        u, plane = jobs[n][2:4]
+        some = pl.ds(0, (side - 1) * side)
+        remote(u.at[some], plane.at[some], job, 5 * n + 1, partner).wait()
+
+        def add(i):
+            x = plane[i].astype(F32)
+            for k in range(1, side):
+                x = x + plane[k * side + i].astype(F32)
+            u[i] = x.astype(BF16)
+
+        each(side, add)
 
         def send(i):
-            to = lax.rem(xy + i + 1, nx)
-            remote(u.at[to], plane.at[xy], job, 4 * n + 1, (dp, zh * nx + to)).start()
-
-        each(nx - 1, send)
-        plane[xy] = u[xy]
+            to = lax.rem(crossed + i + 1, side)
+            remote(
+                u.at[to], plane_b[n].at[crossed], job, 5 * n + 4, along(mine, to)
+            ).start()
+
+        each(side - 1, send)
+        plane_b[n][crossed] = u[crossed]
 
     def plane_add(n):
         u, plane, total, col = jobs[n][2:6]
         count, base, inside, member = zone(n)
-        remote(
-            u.at[pl.ds(0, nx - 1)], plane.at[pl.ds(0, nx - 1)], job, 4 * n + 1, partner
-        ).wait()
+        if n < 2:
+            some = pl.ds(0, side - 1)
+            plane, sources = plane_b[n], side
+            remote(u.at[some], plane.at[some], job, 5 * n + 4, partner).wait()
+        else:
+            some, sources = pl.ds(0, nx - 1), nx
+            remote(u.at[some], plane.at[some], job, 5 * n + 1, partner).wait()
 
         def add(q):
             x = plane[0, q].astype(F32)
-            for i in range(1, nx):
+            for i in range(1, sources):
                 x = x + plane[i, q].astype(F32)
             total[q] = x.astype(BF16)
 
@@ -213,7 +263,7 @@
                 @pl.when((base + i != zh) | (zl != n % 2))
                 def _():
                     device = ((n % 2) * 2 + core, (base + i) * nx + xy)
-                    remote(total.at[i], col.at[z], job, 4 * n + 2, device).start()
+                    remote(total.at[i], col.at[z], job, 5 * n + 2, device).start()
 
             each(count, send)
 
@@ -230,7 +280,7 @@
                 def _():
                     device = (to_dp, (base + i // 4) * nx + xy)
                     slot = col.at[core * 2 * nz + z]
-                    remote(total.at[i // 4], slot, job, 4 * n + 2, device).start()
+                    remote(total.at[i // 4], slot, job, 5 * n + 2, device).start()
 
             each(4 * count, send)
 
@@ -240,7 +290,7 @@
 
     def pieces(n, sem, size):
         some = pl.ds(0, size)
-        return remote(jobs[n][5].at[some], jobs[n][5].at[some], job, 4 * n + sem, partner)
+        return remote(jobs[n][5].at[some], jobs[n][5].at[some], job, 5 * n + sem, partner)
 
     def sum_of(col, start):
         x = col[start].astype(F32)
@@ -258,7 +308,7 @@
             fin[core] = sum_of(col, 0).astype(BF16)
             for d in range(1, 4):
                 device = (lax.rem(dp + d, 4), seq)
-                remote(fin.at[core], fin.at[core], job, 4 * n + 3, device).start()
+                remote(fin.at[core], fin.at[core], job, 5 * n + 3, device).start()
             pieces(n, 2, count - 1).wait_send()
 
         @pl.when(jnp.logical_not(member))
@@ -273,12 +323,12 @@
         def _():
             @pl.when(member)
             def _():
-                remote(fin.at[other], fin.at[other], job, 4 * n + 3, partner).wait_recv()
+                remote(fin.at[other], fin.at[other], job, 5 * n + 3, partner).wait_recv()
                 pieces(n, 3, 3).wait_send()
 
             @pl.when(jnp.logical_not(member))
             def _():
-                remote(fin, fin, job, 4 * n + 3, partner).wait_recv()
+                remote(fin, fin, job, 5 * n + 3, partner).wait_recv()
 
             at = [
                 ((0, slice(0, half)), (1, slice(0, half))),
@@ -337,20 +387,13 @@
             fin[core, k] = (u[k].astype(F32) + near[k].astype(F32)).astype(BF16)
             fin_copy(n, k).start()
 
-    def factor_end(n, wide_sum, store):
+    def factor_end(n, wide_sum):
         fin = facs[n][4]
         for k in range(2):
             fin_copy(n, k).wait()
         for k in range(4):
             wide_sum[k] = fin[k // 2, k % 2].astype(F32)
-        store.start()
-
-    stores = [
-        pltpu.make_async_copy(src, dst, store_sem.at[i])
-        for i, (src, dst) in enumerate(
-            ((res, res_h), (grad, grad_h), (first, first_out), (second, second_out))
-        )
-    ]
+
     for which in range(2):
         wide[which, width:, :] = jnp.zeros((8, half), F32)
 
@@ -444,6 +487,7 @@
             put_rows(c, which, 0, ns // 2)
         pair_copy(c).start()
     factor_start(0, first)
+    side_add(0)
     pair_add(1)
     factor_pair(0, 1)
 
@@ -453,8 +497,8 @@
         grad[a] = (x + y).astype(BF16)
 
     each(4, grads)
-    stores[1].start()
     plane_add(0)
+    side_add(1)
 
     def mix_second(g):
         c, start, size = forward_groups[g]
@@ -524,8 +568,7 @@
         res[p] = x.astype(BF16)
 
     each(4, results)
-    stores[0].start()
-    factor_end(0, first, stores[2])
+    factor_end(0, first)
     plane_add(4)
     column_add(2)
     for n in range(2):
@@ -534,9 +577,7 @@
     finish(2)
     finish_last(3)
     finish_last(4)
-    factor_end(1, second, stores[3])
-    for store in stores:
-        store.wait()
+    factor_end(1, second)
 
 
 def mega_call(nz, nx, *args):
@@ -570,10 +611,6 @@
         vmem((2, 4, rows, half), BF16),
         vmem((2, 4, rows, half), BF16),
         vmem((half, 4 * rows), BF16),
-        vmem((4, rows, width), BF16),
-        vmem((4, rows, width), BF16),
-        vmem((4, rows, rows), F32),
-        vmem((4, rows, rows), F32),
         vmem((3, 4 * rows, half // 3), F32),
         vmem((2, width + 8, half), F32),
     ]
@@ -588,6 +625,7 @@
             vmem((4 * nz if n > 2 else 2 * nz, 16, half), BF16),
             vmem((2, 16, half), BF16),
         ]
+    scratch += [vmem((int(nx**0.5), nz, 16, half), BF16)] * 2
     for _ in range(2):
         scratch += [
             vmem((2, 2, rows, rows), BF16),
@@ -596,22 +634,18 @@
             vmem((2, rows, rows), BF16),
             vmem((2, 2, rows, rows), BF16),
         ]
-    scratch += [sem((count,)) for count in (12, 4, 6, 6, 20, 20, 12, 12)]
+    scratch += [sem((count,)) for count in (12, 6, 6, 25, 25, 12, 12)]
     anywhere = pl.BlockSpec(memory_space=pl.ANY)
     return pl.pallas_call(
         functools.partial(mega, nz, nx),
-        out_shape=(
-            jax.ShapeDtypeStruct((4, rows, width), BF16),
-            jax.ShapeDtypeStruct((4, rows, width), BF16),
-            jax.ShapeDtypeStruct((4, rows, rows), F32),
-            jax.ShapeDtypeStruct((4, rows, rows), F32),
-        )
-        + (jax.ShapeDtypeStruct((12, width), F32),) * 3,
+        out_shape=(vmem((4, rows, width), BF16),) * 2
+        + (vmem((4, rows, rows), F32),) * 2
+        + (vmem((12, width), F32),) * 3,
         in_specs=[anywhere] * 7,
-        out_specs=(anywhere,) * 4 + (pl.BlockSpec(memory_space=vmem),) * 3,
+        out_specs=(pl.BlockSpec(memory_space=vmem),) * 7,
         scratch_shapes=scratch,
         compiler_params=pltpu.CompilerParams(
-            collective_id=0, has_side_effects=True, vmem_limit_bytes=60 * 2**20
+            collective_id=0, has_side_effects=True, vmem_limit_bytes=53 * 2**20
         ),
         cost_estimate=pl.CostEstimate(
             flops=14 * 10**9, bytes_accessed=16 * 10**6, transcendentals=10**6
@@ -620,11 +654,36 @@
     )(*args)
 
 
+def deliver(*refs):
+    sources, targets, sem = refs[:7], refs[7:14], refs[14]
+    copies = []
+    for src, dst in zip(sources, targets):
+        for i in range(src.shape[0] if len(src.shape) == 3 else 1):
+            pair = (src.at[i], dst.at[i]) if len(src.shape) == 3 else (src, dst)
+            copies.append(pltpu.make_async_copy(*pair, sem.at[len(copies)]))
+    for copy in copies:
+        copy.start()
+    for copy in copies:
+        copy.wait()
+
+
+def deliver_call(arrays):
+    return pl.pallas_call(
+        deliver,
+        out_shape=tuple(jax.ShapeDtypeStruct(x.shape, x.dtype) for x in arrays),
+        in_specs=[pl.BlockSpec(memory_space=pltpu.VMEM)] * 7,
+        out_specs=(pl.BlockSpec(memory_space=pl.ANY),) * 7,
+        scratch_shapes=[pltpu.SemaphoreType.DMA((19,))],
+        compiler_params=pltpu.CompilerParams(vmem_limit_bytes=2**20),
+        name="deliver",
+    )(*arrays)
+
+
 def shards(
     nz, nx, tokens, first_factor, second_factor, value_weight, gate_weight, out_weight, cotangent
 ):
     rows, width = 4 * nz * nx, 12 * nz * nx
-    result, grad, first, second, value_sum, gate_sum, out_sum = mega_call(
+    arrays = mega_call(
         nz,
         nx,
         tokens.reshape(4, rows, width),
@@ -635,6 +694,7 @@
         out_weight,
         cotangent.reshape(4, rows, width),
     )
+    result, grad, first, second, value_sum, gate_sum, out_sum = deliver_call(arrays)
     return (
         result.reshape(1, 4 * rows, width),
         grad.reshape(1, 4 * rows, width),

time: 116 us -> 107 us (0.922)
  local copies, waits for them, and re-layouts: 9.01 us -> 0 us
    unnamed x19 -> x0, local copies, waits for them, and re-layouts: 9.01 us -> none
    pallas_call x1 -> x2, Pallas kernels: 106 us -> 106 us  [the longest x1 103 us: mega_call(): pl.pallas_call(functools.partial(mega, nz, nx), out_shape=(vmem((4, rows,...]
where the time goes in v5:
time: 107 us
  Pallas kernels  106 us (99%)
    pallas_call x1, Pallas kernels, mega_call(): pl.pallas_call(functools.partial(mega, nz, nx), out_shape=(vmem((4, rows,...  103 us
    pallas_call x1, Pallas kernels, deliver_call(): pl.pallas_call(deliver, out_shape=tuple((jax.ShapeDtypeStruct(x.shape, x....  2.51 us

profile of v5, /device:TPU:1, one launch (start us, length us, event | category | flops | bytes accessed | tf_op | source)
XLA Modules:
  0.0 106.5 jit_solution(706849565105376113)
XLA Ops:
  0.6 103.3 %mixing.1 = (bf16[4,256,768]{2,1,0:T(8,128)(2,1)S(1)}, bf16[4,256,768]{2,1,0:T(8,128)(2,1)S(1)}, f32[4,256,256]{2,1,0:T(8,128)S(1)}, f32[4,256,256]{2,1,0:T(8,12...) custom-call(bf16[4,256,768]{2,1,0:T(8,128)(2,1)} %bitcast.4, ...), custom_call_target="tpu_custom_call" | custom-call | flops 14000000000 | bytes 16000000 | tf_op jit(solution)/shard_map/mixing/pallas_call | solution.py:639
  104.0 2.5 %deliver.1 = (bf16[4,256,768]{2,1,0:T(8,128)(2,1)}, bf16[4,256,768]{2,1,0:T(8,128)(2,1)}, f32[4,256,256]{2,1,0:T(8,128)}, f32[4,256,256]{2,1,0:T(8,128)}, f32[12...) custom-call(bf16[4,256,768]{2,1,0:T(8,128)(2,1)S(1)} %get-tuple-element.21.refs_0_, ...), custom_call_target="tpu_custom_call" | custom-call | tf_op jit(solution)/shard_map/deliver/pallas_call | solution.py:671

commit v6 on v5

--- a/solution.py
+++ b/solution.py
@@ -358,10 +358,12 @@
         own, pair = facs[n][:2]
         return remote(own.at[other, k], pair.at[k], fac, 6 * n + k, partner)
 
-    def factor_start(n, source):
+    def factor_start(n, source, before=None):
         own = facs[n][0]
         for k in range(2):
             for h in range(2):
+                if before is not None:
+                    before(2 * h + k)
                 own[h, k] = source[2 * h + k].astype(BF16)
             factor_copy(n, k).start()
 
@@ -452,13 +454,13 @@
 
     for c in range(2):
         groups = [g for g in range(3) if back_groups[g][0] == c]
+        if c == 1:
+            pair_add(0)
         for g in groups:
             back_copy(g).wait_send()
         for g in range(3):
             if forward_groups[g][0] == c:
                 send_all(fsend[g], frecv[g], 3 + g)
-        if c == 1:
-            pair_add(0)
         for g in groups:
             back_copy(g).wait_recv()
             from_messages(brecv[g], *back_groups[g][1:])
@@ -500,12 +502,13 @@
     plane_add(0)
     side_add(1)
 
+    def take(g):
+        forward_copy(g).wait_recv()
+        from_messages(frecv[g], *forward_groups[g][1:])
+
     def mix_second(g):
         c, start, size = forward_groups[g]
         cols = slice(start, start + size)
-        forward_copy(g).wait_recv()
-        from_messages(frecv[g], start, size)
-
         def inner(p):
             sec[c, p, :, cols] = dot(sf[p], got[p, :, cols]).astype(BF16)
 
@@ -516,19 +519,19 @@
             right = cot[:, :, which * half : (which + 1) * half].reshape(4 * rows, half)
             wide[which, cols, :] = dot(sec_t[cols, :], right)
 
-    def grow_second(g):
+    def grow(g, p):
         c, start, size = forward_groups[g]
         cols = slice(start, start + size)
-
-        def outer(p):
-            more = dot_cols(bs[c, p, :, cols], got[p, :, cols])
-            if g == 0:
-                second[p] = more
-            else:
-                second[p] = second[p] + more
-
-        each(4, outer)
-
+        more = dot_cols(bs[c, p, :, cols], got[p, :, cols])
+        if g == 0:
+            second[p] = more
+        else:
+            second[p] = second[p] + more
+
+    def grow_second(g):
+        each(4, functools.partial(grow, g))
+
+    take(0)
     mix_second(0)
     for which in range(2):
         put_rows(2, which, 0, ns // 4)
@@ -538,6 +541,7 @@
     pair_add(2)
     pairs = ns // 8
     early = 2 * lanes // 24 - pairs
+    take(1)
     mix_second(1)
     for which in range(2):
         put_rows(3, which, 0, pairs)
@@ -552,14 +556,14 @@
     plane_add(2)
     column_add(0)
     column_add(1)
+    take(2)
+    factor_start(1, second, functools.partial(grow, 2))
     mix_second(2)
     for which in range(2):
         put_rows(4, which, early, pairs, pairs)
     pair_copy(4).start()
-    grow_second(2)
-    factor_start(1, second)
+    factor_pair(1, 2)
     pair_add(4)
-    factor_pair(1, 2)
     plane_add(3)
     factor_near(0)
 

time: 107 us -> 104 us (0.972)
  Pallas kernels: 106 us -> 103 us
    pallas_call x1, Pallas kernels: 103 us -> 100 us  [mega_call(): pl.pallas_call(functools.partial(mega, nz, nx), out_shape=(vmem((4, rows,...]
where the time goes in v6:
time: 104 us
  Pallas kernels  103 us (99%)
    pallas_call x1, Pallas kernels, mega_call(): pl.pallas_call(functools.partial(mega, nz, nx), out_shape=(vmem((4, rows,...  100 us
    pallas_call x1, Pallas kernels, deliver_call(): pl.pallas_call(deliver, out_shape=tuple((jax.ShapeDtypeStruct(x.shape, x....  2.51 us

profile of v6, /device:TPU:1, one launch (start us, length us, event | category | flops | bytes accessed | tf_op | source)
XLA Modules:
  0.0 103.5 jit_solution(14817117691116939875)
XLA Ops:
  0.6 100.3 %mixing.1 = (bf16[4,256,768]{2,1,0:T(8,128)(2,1)S(1)}, bf16[4,256,768]{2,1,0:T(8,128)(2,1)S(1)}, f32[4,256,256]{2,1,0:T(8,128)S(1)}, f32[4,256,256]{2,1,0:T(8,12...) custom-call(bf16[4,256,768]{2,1,0:T(8,128)(2,1)} %bitcast.4, ...), custom_call_target="tpu_custom_call" | custom-call | flops 14000000000 | bytes 16000000 | tf_op jit(solution)/shard_map/mixing/pallas_call | solution.py:643
  101.0 2.5 %deliver.1 = (bf16[4,256,768]{2,1,0:T(8,128)(2,1)}, bf16[4,256,768]{2,1,0:T(8,128)(2,1)}, f32[4,256,256]{2,1,0:T(8,128)}, f32[4,256,256]{2,1,0:T(8,128)}, f32[12...) custom-call(bf16[4,256,768]{2,1,0:T(8,128)(2,1)S(1)} %get-tuple-element.21.refs_0_, ...), custom_call_target="tpu_custom_call" | custom-call | tf_op jit(solution)/shard_map/deliver/pallas_call | solution.py:675

commit v7 on v6

--- a/solution.py
+++ b/solution.py
@@ -72,7 +72,7 @@
     loads = [
         pltpu.make_async_copy(src, dst, load_sem.at[i]) for i, (src, dst) in enumerate(parts)
     ]
-    for i in (0, 1, 4, 5, 6, 7, 2, 3):
+    for i in (1, 4, 0, 5, 6, 7):
         loads[i].start()
 
     barrier = pltpu.get_barrier_semaphore()
@@ -413,9 +413,10 @@
             for p in range(4):
                 sf_t[p] = sf[p].T
                 loads[4 + p].wait()
+                if p == 1:
+                    for load in loads[2:4] + loads[8:]:
+                        load.start()
                 back(p)
-            for load in loads[8:]:
-                load.start()
         else:
             each(4, back)
         to_messages(bsend[g], 0, size)

time: 104 us -> 103 us (level)
  no operation moved by 1% of the time
where the time goes in v7:
time: 103 us
  Pallas kernels  102 us (99%)
    pallas_call x1, Pallas kernels, mega_call(): pl.pallas_call(functools.partial(mega, nz, nx), out_shape=(vmem((4, rows,...  99.8 us
    pallas_call x1, Pallas kernels, deliver_call(): pl.pallas_call(deliver, out_shape=tuple((jax.ShapeDtypeStruct(x.shape, x....  2.51 us

profile of v7, /device:TPU:1, one launch (start us, length us, event | category | flops | bytes accessed | tf_op | source)
XLA Modules:
  0.0 103.0 jit_solution(11943933060749879091)
XLA Ops:
  0.6 99.8 %mixing.1 = (bf16[4,256,768]{2,1,0:T(8,128)(2,1)S(1)}, bf16[4,256,768]{2,1,0:T(8,128)(2,1)S(1)}, f32[4,256,256]{2,1,0:T(8,128)S(1)}, f32[4,256,256]{2,1,0:T(8,12...) custom-call(bf16[4,256,768]{2,1,0:T(8,128)(2,1)} %bitcast.4, ...), custom_call_target="tpu_custom_call" | custom-call | flops 14000000000 | bytes 16000000 | tf_op jit(solution)/shard_map/mixing/pallas_call | solution.py:644
  100.5 2.5 %deliver.1 = (bf16[4,256,768]{2,1,0:T(8,128)(2,1)}, bf16[4,256,768]{2,1,0:T(8,128)(2,1)}, f32[4,256,256]{2,1,0:T(8,128)}, f32[4,256,256]{2,1,0:T(8,128)}, f32[12...) custom-call(bf16[4,256,768]{2,1,0:T(8,128)(2,1)S(1)} %get-tuple-element.21.refs_0_, ...), custom_call_target="tpu_custom_call" | custom-call | tf_op jit(solution)/shard_map/deliver/pallas_call | solution.py:676

commit v8 on v7

--- a/solution.py
+++ b/solution.py
@@ -576,10 +576,9 @@
     factor_end(0, first)
     plane_add(4)
     column_add(2)
-    for n in range(2):
+    factor_near(1)
+    for n in range(3):
         finish(n)
-    factor_near(1)
-    finish(2)
     finish_last(3)
     finish_last(4)
     factor_end(1, second)

time: 103 us -> 103 us (level)
  no operation moved by 1% of the time
where the time goes in v8:
time: 103 us
  Pallas kernels  102 us (99%)
    pallas_call x1, Pallas kernels, mega_call(): pl.pallas_call(functools.partial(mega, nz, nx), out_shape=(vmem((4, rows,...  99.8 us
    pallas_call x1, Pallas kernels, deliver_call(): pl.pallas_call(deliver, out_shape=tuple((jax.ShapeDtypeStruct(x.shape, x....  2.51 us

profile of v8, /device:TPU:1, one launch (start us, length us, event | category | flops | bytes accessed | tf_op | source)
XLA Modules:
  0.0 103.0 jit_solution(3170827515266115111)
XLA Ops:
  0.6 99.8 %mixing.1 = (bf16[4,256,768]{2,1,0:T(8,128)(2,1)S(1)}, bf16[4,256,768]{2,1,0:T(8,128)(2,1)S(1)}, f32[4,256,256]{2,1,0:T(8,128)S(1)}, f32[4,256,256]{2,1,0:T(8,12...) custom-call(bf16[4,256,768]{2,1,0:T(8,128)(2,1)} %bitcast.4, ...), custom_call_target="tpu_custom_call" | custom-call | flops 14000000000 | bytes 16000000 | tf_op jit(solution)/shard_map/mixing/pallas_call | solution.py:643
  100.5 2.5 %deliver.1 = (bf16[4,256,768]{2,1,0:T(8,128)(2,1)}, bf16[4,256,768]{2,1,0:T(8,128)(2,1)}, f32[4,256,256]{2,1,0:T(8,128)}, f32[4,256,256]{2,1,0:T(8,128)}, f32[12...) custom-call(bf16[4,256,768]{2,1,0:T(8,128)(2,1)S(1)} %get-tuple-element.21.refs_0_, ...), custom_call_target="tpu_custom_call" | custom-call | tf_op jit(solution)/shard_map/deliver/pallas_call | solution.py:675
